TPU v7x, 32 devices: a whole 2x2x4 slice. The times are simulated.
32 devices in a mesh: pix: 8 (over z, x), feat: 4 (over y, core).
Axes of the slice: x: 2, y: 2, z: 4, core: 2. Of those that a mesh axis runs over, the one named last changes fastest.
Arguments:
- mass_bin: int32 [32768, 256], P(('pix', 'feat')), may hold values from 0 to 255
- mobility_bin: int32 [32768, 256], P(('pix', 'feat')), may hold values from 0 to 15
- intensity: bfloat16 [32768, 256], P(('pix', 'feat')), may hold values from 10 to 4000, as said below
- basis_init: float32 [32768, 64], P(('pix', 'feat')), may hold values from 0.1 to 1
- profile_init: float32 [64, 4096], P(None, 'feat'), may hold values from 0.1 to 1
Outputs:
- basis: float32 [32768, 64], P(('pix', 'feat'))
- profiles: float32 [64, 4096], P(None, 'feat')
Inputs may be any that keep to these rules, and one draw needn't show every extreme that they name: `intensity`: positive peak intensities.
All inputs are finite; a program needn't handle non-finite values.
Results may differ from a plain program's by a relative error of at most 0.00045.
Values may be sent and summed in bfloat16 or wider, within the bound.
A program may use at most 64 MiB of HBM per device.

v0:
```python
import math

import jax
import jax.numpy as jnp
from jax import lax
from jax.sharding import PartitionSpec as P

MZ = 256
MOB = 16
PEAKS = 256
ITERS = 2


EPS = 1e-06


def bin_block(args):
    mass, mobility, weight = args
    mass_hot = (mass[:, :, None] == jnp.arange(MZ, dtype=jnp.int32)[None, None, :]).astype(
        jnp.bfloat16
    ) * weight[:, :, None]
    mobility_hot = (mobility[:, :, None] == jnp.arange(MOB, dtype=jnp.int32)[None, None, :]).astype(
        jnp.bfloat16
    )
    dense = jnp.einsum("pkb,pkm->pbm", mobility_hot, mass_hot, preferred_element_type=jnp.float32)
    return dense.reshape(mass.shape[0], MZ * MOB).astype(jnp.bfloat16)


def local(mass_bin, mobility_bin, intensity, basis_init, profile_init):
    rows = mass_bin.shape[0]
    block = math.gcd(rows, 32)
    count = rows // block
    spectra = lax.map(
        bin_block,
        (
            mass_bin.reshape(count, block, PEAKS),
            mobility_bin.reshape(count, block, PEAKS),
            intensity.reshape(count, block, PEAKS),
        ),
    )
    spectra = spectra.reshape(rows, MZ * MOB)
    highest = lax.Precision.HIGHEST
    basis, profiles = (basis_init, profile_init)
    for step in range(ITERS):
        partial_h = lax.dot_general(
            basis.astype(jnp.bfloat16),
            spectra,
            (((0,), (0,)), ((), ())),
            preferred_element_type=jnp.float32,
        )
        partial_gram = lax.dot_general(
            basis,
            basis,
            (((0,), (0,)), ((), ())),
            precision=highest,
            preferred_element_type=jnp.float32,
        )
        shared = lax.psum_scatter(partial_h, "feat", scatter_dimension=1, tiled=True)
        numer_h = lax.psum(shared, "pix")
        gram_w = lax.psum(partial_gram, ("pix", "feat"))
        profiles = (
            profiles
            * numer_h
            / (
                jnp.dot(gram_w, profiles, precision=highest, preferred_element_type=jnp.float32)
                + EPS
            )
        )
        numer_w = lax.dot_general(
            spectra,
            lax.all_gather(profiles.astype(jnp.bfloat16), "feat", axis=1, tiled=True),
            (((1,), (1,)), ((), ())),
            preferred_element_type=jnp.float32,
        )
        local_gram = lax.dot_general(
            profiles,
            profiles,
            (((1,), (1,)), ((), ())),
            precision=highest,
            preferred_element_type=jnp.float32,
        )
        gram_h = lax.psum(local_gram, "feat")
        basis = (
            basis
            * numer_w
            / (jnp.dot(basis, gram_h, precision=highest, preferred_element_type=jnp.float32) + EPS)
        )
    return (basis, profiles)


def solution(mesh):
    return jax.shard_map(
        local,
        mesh=mesh,
        in_specs=(
            P(("pix", "feat"), None),
            P(("pix", "feat"), None),
            P(("pix", "feat"), None),
            P(("pix", "feat"), None),
            P(None, "feat"),
        ),
        out_specs=(P(("pix", "feat"), None), P(None, "feat")),
        check_vma=False,
    )
```

profile of v0, /device:TPU:0, one launch (start us, length us, event | category | flops | bytes accessed | tf_op | source)
XLA Modules:
  0.0 472.6 jit_solution(7452351486102665172)
XLA Ops:
  7.2 192.9 %while.10 = (s32[]{:T(128)}, bf16[32,32,4096]{2,1,0:T(8,128)(2,1)}, s32[32,32,256]{2,1,0:T(8,128)}, s32[32,32,256]{2,1,0:T(8,128)}, bf16[32,32,256]{2,1,0:T(8,128)(2,1)}, /*index=5*/s32[]{:T(128)}) while((s32[]{:T(128)}, bf16[32,32,4096]{2,1,0:T(8,128)(2,1)}, s32[32,32,256]{2,1,0:T(8,128)}, s32[32,32,256]{2,1,0:T(8,128)}, ...), condition=%wide.region_1.2_spmd, body=%wide.region_0.1_spmd.sunk | while | flops 71565312 | bytes 1557069 | solution.py:33
  8.8 3.7 fusion.50
  14.8 3.7 fusion.50
  20.8 3.7 fusion.50
  26.8 3.7 fusion.50
  32.9 3.7 fusion.50
  38.9 3.7 fusion.50
  44.9 3.7 fusion.50
  51.0 3.7 fusion.50
  57.0 3.7 fusion.50
  63.0 3.7 fusion.50
  69.0 3.7 fusion.50
  75.1 3.7 fusion.50
  81.1 3.7 fusion.50
  87.1 3.7 fusion.50
  93.2 3.7 fusion.50
  99.2 3.7 fusion.50
  105.2 3.7 fusion.50
  111.2 3.7 fusion.50
  117.2 3.7 fusion.50
  123.3 3.7 fusion.50
  129.3 3.7 fusion.50
  135.3 3.7 fusion.50
  141.4 3.7 fusion.50
  147.4 3.7 fusion.50
  153.4 3.7 fusion.50
  159.4 3.7 fusion.50
  165.5 3.7 fusion.50
  171.5 3.7 fusion.50
  177.5 3.7 fusion.50
  183.6 3.7 fusion.50
  189.6 3.7 fusion.50
  195.6 3.7 fusion.50
  200.1 6.1 %convolution_bitcast_fusion = f32[64,4096]{1,0:T(8,128)} fusion(bf16[1024,4096]{1,0:T(8,128)(2,1)} %bitcast.42, f32[1024,64]{0,1:T(8,128)S(1)} %copy-done), kind=kOutput, calls=%fused_computation.14 | convolution fusion | flops 536936448 | bytes 9699328 | tf_op jit(solution)/shard_map/dot_general | solution.py:45
  206.2 27.7 %reduce-scatter.3.cloned.1.call-done = f32[64,1024]{1,0:T(8,128)} async-done(((f32[64,4096]{1,0:T(8,128)}), f32[64,1024]{1,0:T(8,128)}) %reduce-scatter.3.cloned.1.call-update) | async-done | bytes 262160 | tf_op jit(solution)/shard_map/reduce_scatter | solution.py:58
  234.4 39.6 %psum.43 = f32[64,64]{1,0:T(8,128)S(1)} all-reduce(f32[64,64]{1,0:T(8,128)S(1)} %fusion.21), channel_id=1, replica_groups=mesh['pix'=8,'feat'=4] {'pix','feat'}, use_global_device_ids=true, to_apply=%region_4.5 | all-reduce | flops 4096 | bytes 32768 | tf_op jit(solution)/shard_map/psum | solution.py:60
  274.0 34.3 %all-reduce.3.cloned.1.call-done = f32[64,1024]{1,0:T(8,128)} async-done(((f32[64,1024]{1,0:T(8,128)}), f32[64,1024]{1,0:T(8,128)}) %all-reduce.3.cloned.1.call-update) | async-done | bytes 262160 | tf_op jit(solution)/shard_map/psum | solution.py:59
  308.3 1.3 fusion.19
  309.7 7.1 %all_gather.6 = bf16[64,4096]{1,0:T(8,128)(2,1)S(1)} all-gather(bf16[64,1024]{1,0:T(8,128)(2,1)S(1)} %get-tuple-element.42), channel_id=1, replica_groups=mesh['pix'=8,'feat'=4] {'feat'}, dimensions={1}, use_global_device_ids=true | all-gather | bytes 655360 | tf_op jit(solution)/shard_map/all_gather | solution.py:71
  316.8 6.0 %convolution_multiply_fusion.1 = f32[1024,64]{0,1:T(8,128)S(1)} fusion(f32[1024,64]{0,1:T(8,128)S(1)} %copy-done, bf16[1024,4096]{1,0:T(8,128)(2,1)} %bitcast.43, bf16[64,4096]{1,0:T(8,128)(2,1)S(1)} %all_gather.6), kind=kOutput, calls=%fused_computation.25 | convolution fusion | flops 536936448 | bytes 9437184 | tf_op jit(solution)/shard_map/dot_general | solution.py:69
  323.2 10.9 %psum.44 = f32[64,64]{1,0:T(8,128)S(1)} all-reduce(f32[64,64]{1,0:T(8,128)S(1)} %fusion.22), channel_id=1, replica_groups=mesh['pix'=8,'feat'=4] {'feat'}, use_global_device_ids=true, to_apply=%region_5.6 | all-reduce | flops 4096 | bytes 32768 | tf_op jit(solution)/shard_map/psum | solution.py:82
  334.6 6.0 %fusion.16 = f32[64,4096]{1,0:T(8,128)} fusion(bf16[1024,4096]{1,0:T(8,128)(2,1)} %bitcast.44, f32[1024,64]{0,1:T(8,128)S(1)} %fusion.14), kind=kOutput, calls=%fused_computation.26 | convolution fusion | flops 536936448 | bytes 9699328 | tf_op jit(solution)/shard_map/dot_general | solution.py:45
  340.7 24.0 %reduce-scatter.5.cloned.1.call-done = f32[64,1024]{1,0:T(8,128)} async-done(((f32[64,4096]{1,0:T(8,128)}), f32[64,1024]{1,0:T(8,128)}) %reduce-scatter.5.cloned.1.call-update) | async-done | bytes 262160 | tf_op jit(solution)/shard_map/reduce_scatter | solution.py:58
  365.1 39.6 %psum.46 = f32[64,64]{1,0:T(8,128)S(1)} all-reduce(f32[64,64]{1,0:T(8,128)S(1)} %fusion.23), channel_id=1, replica_groups=mesh['pix'=8,'feat'=4] {'pix','feat'}, use_global_device_ids=true, to_apply=%region_8.9 | all-reduce | flops 4096 | bytes 32768 | tf_op jit(solution)/shard_map/psum | solution.py:60
  404.7 34.3 %all-reduce.5.cloned.1.call-done = f32[64,1024]{1,0:T(8,128)} async-done(((f32[64,1024]{1,0:T(8,128)}), f32[64,1024]{1,0:T(8,128)}) %all-reduce.5.cloned.1.call-update) | async-done | bytes 262160 | tf_op jit(solution)/shard_map/psum | solution.py:59
  440.4 7.2 %all_gather.7 = bf16[64,4096]{1,0:T(8,128)(2,1)S(1)} all-gather(bf16[64,1024]{1,0:T(8,128)(2,1)S(1)} %get-tuple-element.44), channel_id=1, replica_groups=mesh['pix'=8,'feat'=4] {'feat'}, dimensions={1}, use_global_device_ids=true | all-gather | bytes 655360 | tf_op jit(solution)/shard_map/all_gather | solution.py:71
  447.6 6.0 %convolution_multiply_fusion = f32[1024,64]{0,1:T(8,128)S(1)} fusion(f32[1024,64]{0,1:T(8,128)S(1)} %fusion.14, bf16[1024,4096]{1,0:T(8,128)(2,1)} %bitcast.45, bf16[64,4096]{1,0:T(8,128)(2,1)S(1)} %all_gather.7), kind=kOutput, calls=%fused_computation.24 | convolution fusion | flops 536936448 | bytes 9437184 | tf_op jit(solution)/shard_map/dot_general | solution.py:69
  454.0 10.9 %psum.47 = f32[64,64]{1,0:T(8,128)S(1)} all-reduce(f32[64,64]{1,0:T(8,128)S(1)} %fusion.24), channel_id=1, replica_groups=mesh['pix'=8,'feat'=4] {'feat'}, use_global_device_ids=true, to_apply=%region_9.10 | all-reduce | flops 4096 | bytes 32768 | tf_op jit(solution)/shard_map/psum | solution.py:82
  (150 shorter events, 80.0 us)
Async XLA Ops:
  7.2 226.8 %reduce-scatter.3.cloned.1.call-start = ((), (), s32[]{:S(2)}) async-start(), calls=%async_computation.2 | async-start | bytes 1310720 | tf_op jit(solution)/shard_map/reduce_scatter | solution.py:58
  7.2 192.9 %copy-start = (f32[1024,64]{0,1:T(8,128)S(1)}, f32[1024,64]{0,1:T(8,128)}, u32[]{:S(2)}) copy-start(f32[1024,64]{0,1:T(8,128)} %param.10) | copy-start | bytes 786436
  200.1 108.2 %copy-start.2 = (f32[64,1024]{1,0:T(8,128)S(1)}, f32[64,1024]{1,0:T(8,128)}, u32[]{:S(2)}) copy-start(f32[64,1024]{1,0:T(8,128)} %param.11) | copy-start | bytes 786436
  206.2 102.1 %all-reduce.3.cloned.1.call-start = ((), (), s32[]{:S(2)}) async-start(), calls=%async_computation.3 | async-start | bytes 524288 | tf_op jit(solution)/shard_map/psum | solution.py:59
  234.0 130.8 %reduce-scatter.5.cloned.1.call-start = ((), (), s32[]{:S(2)}) async-start(), calls=%async_computation.4 | async-start | bytes 1310720 | tf_op jit(solution)/shard_map/reduce_scatter | solution.py:58
  340.7 98.4 %all-reduce.5.cloned.1.call-start = ((), (), s32[]{:S(2)}) async-start(), calls=%async_computation.5 | async-start | bytes 524288 | tf_op jit(solution)/shard_map/psum | solution.py:59
  440.4 25.7 %copy-start.1 = (f32[64,1024]{1,0:T(8,128)}, f32[64,1024]{1,0:T(8,128)S(1)}, u32[]{:S(2)}) copy-start(f32[64,1024]{1,0:T(8,128)S(1)} %get-tuple-element.45) | copy-start | bytes 786436
Sparse Core Ops, SparseCore 0:
  206.3 27.5 reduce-scatter.2
  237.7 70.6 all-reduce.2
  340.8 23.9 reduce-scatter.4
  368.3 70.6 all-reduce.4
where the time goes:
time: 477 us; the launch traced here: 473 us
  matrix products  147 us (31%)
  waiting for transfers between devices  120 us (25%)
  blocking collectives  115 us (24%)
  local copies, waits for them, and re-layouts  75.5 us (16%)
  between operations  13.9 us (3%)
    dot_general x32, matrix products, bin_block(): jnp.einsum('pkb,pkm->pbm', mobility_hot, mass_hot, preferred_element_type...  117 us
    psum x2, blocking collectives, local(): gram_w = lax.psum(partial_gram, ('pix', 'feat'))  79.2 us
    psum x2, waiting for transfers between devices, local(): numer_h = lax.psum(shared, 'pix')  68.7 us
    reduce_scatter x2, waiting for transfers between devices, local(): lax.psum_scatter(partial_h, 'feat', scatter_dimension=1, tiled=True)  51.7 us
    eq x32, local copies, waits for them, and re-layouts, bin_block(): mass[:, :, None] == jnp.arange(MZ, dtype=jnp.int32)[None, None, :]  25 us
    dynamic_update_slice x32, local copies, waits for them, and re-layouts, local(): lax.map(bin_block, (mass_bin.reshape(count, block, PEAKS), mobility_bin.r...  23.4 us
    mul x32, local copies, waits for them, and re-layouts, bin_block(): (mass[:, :, None] == jnp.arange(MZ, dtype=jnp.int32)[None, None, :]).asty...  23 us
    psum x2, blocking collectives, local(): gram_h = lax.psum(local_gram, 'feat')  21.9 us
  transfers between devices with their start and end apart: 4, of which 4 were waited for; matrix products, arithmetic and copies ran while one was open for 0% of the time, Pallas kernels for 0%

commit v1 on v0

--- a/solution.py
+++ b/solution.py
@@ -1,44 +1,73 @@
-import math
-
 import jax
 import jax.numpy as jnp
 from jax import lax
+from jax.experimental import pallas as pl
+from jax.experimental.pallas import tpu as pltpu
 from jax.sharding import PartitionSpec as P
 
+LANES = 128
 MZ = 256
 MOB = 16
-PEAKS = 256
+HI = MZ * MOB // LANES
+GROUP = 16
 ITERS = 2
-
-
 EPS = 1e-06
 
 
-def bin_block(args):
-    mass, mobility, weight = args
-    mass_hot = (mass[:, :, None] == jnp.arange(MZ, dtype=jnp.int32)[None, None, :]).astype(
-        jnp.bfloat16
-    ) * weight[:, :, None]
-    mobility_hot = (mobility[:, :, None] == jnp.arange(MOB, dtype=jnp.int32)[None, None, :]).astype(
-        jnp.bfloat16
-    )
-    dense = jnp.einsum("pkb,pkm->pbm", mobility_hot, mass_hot, preferred_element_type=jnp.float32)
-    return dense.reshape(mass.shape[0], MZ * MOB).astype(jnp.bfloat16)
+def bin_kernel(mass_ref, mobility_ref, weight_ref, out_ref, hi_ref, lo_ref, value_ref, dense_ref):
+    rows, peaks = mass_ref.shape
+    mass = mass_ref[...]
+    hi_ref[...] = (mobility_ref[...] * (MZ // LANES) + mass // LANES).astype(jnp.float32)
+    lo_ref[...] = (mass % LANES).astype(jnp.float32)
+    value_ref[...] = weight_ref[...].astype(jnp.float32)
+    hi_iota = lax.broadcasted_iota(jnp.int32, (HI, peaks), 0).astype(jnp.float32).astype(jnp.bfloat16)
+    lo_iota = lax.broadcasted_iota(jnp.int32, (LANES, peaks), 0).astype(jnp.float32).astype(jnp.bfloat16)
+
+    def spread(ref, p, count):
+        return jnp.broadcast_to(ref[pl.ds(p, 1), :], (count, peaks)).astype(jnp.bfloat16)
+
+    def group(g, _):
+        base = pl.multiple_of(g * GROUP, GROUP)
+        for i in range(GROUP):
+            p = base + i
+            left = jnp.where(
+                spread(hi_ref, p, HI) == hi_iota, spread(value_ref, p, HI), jnp.bfloat16(0)
+            )
+            right = jnp.where(
+                spread(lo_ref, p, LANES) == lo_iota, jnp.bfloat16(1), jnp.bfloat16(0)
+            )
+            dense_ref[pl.ds(i, HI, stride=GROUP), :] = lax.dot_general(
+                left, right, (((1,), (1,)), ((), ())), preferred_element_type=jnp.float32
+            )
+        for h in range(HI):
+            out_ref[pl.ds(base, GROUP), h * LANES : (h + 1) * LANES] = dense_ref[
+                h * GROUP : (h + 1) * GROUP, :
+            ].astype(jnp.bfloat16)
+        return 0
+
+    lax.fori_loop(0, rows // GROUP, group, 0)
+
+
+def bin_peaks(mass, mobility, weight):
+    rows, peaks = mass.shape
+    block = 128
+    spec = pl.BlockSpec((block, peaks), lambda i: (i, 0))
+    return pl.pallas_call(
+        bin_kernel,
+        out_shape=jax.ShapeDtypeStruct((rows, MZ * MOB), jnp.bfloat16),
+        grid=(rows // block,),
+        in_specs=[spec] * 3,
+        out_specs=pl.BlockSpec((block, MZ * MOB), lambda i: (i, 0)),
+        scratch_shapes=[pltpu.VMEM((block, peaks), jnp.float32)] * 3
+        + [pltpu.VMEM((HI * GROUP, LANES), jnp.float32)],
+        cost_estimate=pl.CostEstimate(
+            flops=2 * rows * peaks * MZ * MOB, bytes_accessed=rows * (peaks * 10 + MZ * MOB * 2), transcendentals=0
+        ),
+    )(mass, mobility, weight)
 
 
 def local(mass_bin, mobility_bin, intensity, basis_init, profile_init):
-    rows = mass_bin.shape[0]
-    block = math.gcd(rows, 32)
-    count = rows // block
-    spectra = lax.map(
-        bin_block,
-        (
-            mass_bin.reshape(count, block, PEAKS),
-            mobility_bin.reshape(count, block, PEAKS),
-            intensity.reshape(count, block, PEAKS),
-        ),
-    )
-    spectra = spectra.reshape(rows, MZ * MOB)
+    spectra = bin_peaks(mass_bin, mobility_bin, intensity)
     highest = lax.Precision.HIGHEST
     basis, profiles = (basis_init, profile_init)
     for step in range(ITERS):

time: 477 us -> 314 us (0.66)
  matrix products: 147 us -> 29.8 us
  local copies, waits for them, and re-layouts: 75.5 us -> 0.01 us
  Pallas kernels: 0 us -> 33.8 us
    dot_general x32 -> x0, matrix products: 117 us -> none  [bin_block(): jnp.einsum('pkb,pkm->pbm', mobility_hot, mass_hot, preferred_element_type...]
    pallas_call x0 -> x1, Pallas kernels: none -> 33.8 us  [bin_peaks(): pl.pallas_call(bin_kernel, out_shape=jax.ShapeDtypeStruct((rows, MZ * MOB...]
    eq x32 -> x0, local copies, waits for them, and re-layouts: 25 us -> none  [bin_block(): mass[:, :, None] == jnp.arange(MZ, dtype=jnp.int32)[None, None, :]]
    dynamic_update_slice x32 -> x0, local copies, waits for them, and re-layouts: 23.4 us -> none  [local(): lax.map(bin_block, (mass_bin.reshape(count, block, PEAKS), mobility_bin.r...]
    mul x32 -> x0, local copies, waits for them, and re-layouts: 23 us -> none  [bin_block(): (mass[:, :, None] == jnp.arange(MZ, dtype=jnp.int32)[None, None, :]).asty...]
where the time goes in v1:
time: 314 us
  waiting for transfers between devices  120 us (38%)
  blocking collectives  115 us (37%)
  Pallas kernels  33.8 us (11%)
  matrix products  29.8 us (9%)
  between operations  13.9 us (4%)
    psum x2, blocking collectives, local(): gram_w = lax.psum(partial_gram, ('pix', 'feat'))  79.2 us
    psum x2, waiting for transfers between devices, local(): numer_h = lax.psum(shared, 'pix')  68.7 us
    reduce_scatter x2, waiting for transfers between devices, local(): lax.psum_scatter(partial_h, 'feat', scatter_dimension=1, tiled=True)  51.7 us
    pallas_call x1, Pallas kernels, bin_peaks(): pl.pallas_call(bin_kernel, out_shape=jax.ShapeDtypeStruct((rows, MZ * MOB...  33.8 us
    psum x2, blocking collectives, local(): gram_h = lax.psum(local_gram, 'feat')  21.9 us
    all_gather x2, blocking collectives, local(): lax.all_gather(profiles.astype(jnp.bfloat16), 'feat', axis=1, tiled=True)  14.3 us
    dot_general x2, matrix products, local(): lax.dot_general(basis.astype(jnp.bfloat16), spectra, (((0,), (0,)), ((),...  12.1 us
    dot_general x2, matrix products, local(): lax.dot_general(spectra, lax.all_gather(profiles.astype(jnp.bfloat16), 'f...  12.1 us
  transfers between devices with their start and end apart: 4, of which 4 were waited for; matrix products, arithmetic and copies ran while one was open for 0% of the time, Pallas kernels for 0%

profile of v1, /device:TPU:0, one launch (start us, length us, event | category | flops | bytes accessed | tf_op | source)
XLA Modules:
  0.0 313.5 jit_solution(7256095688114518212)
XLA Ops:
  7.2 0.0 copy-start
  7.2 0.0 reduce-scatter.3.cloned.1.call-start
  7.2 33.8 %shard_map.68 = bf16[1024,4096]{1,0:T(8,128)(2,1)} custom-call(s32[1024,256]{1,0:T(8,128)} %mass_ref.1, s32[1024,256]{1,0:T(8,128)} %mobility_ref.1, bf16[1024,256]{1,0:T(8,128)(2,1)} %weight_ref.1), custom_call_target="tpu_custom_call" | custom-call | flops 2147483648 | bytes 11010048 | tf_op jit(solution)/shard_map/pallas_call | solution.py:55
  41.0 0.0 copy-done
  41.0 0.0 copy-start.2
  41.0 6.1 %convolution_bitcast_fusion = f32[64,4096]{1,0:T(8,128)} fusion(bf16[1024,4096]{1,0:T(8,128)(2,1)} %shard_map.68, f32[1024,64]{0,1:T(8,128)S(1)} %copy-done), kind=kOutput, calls=%fused_computation | convolution fusion | flops 536936448 | bytes 9699328 | tf_op jit(solution)/shard_map/dot_general | solution.py:74
  47.1 0.0 reduce-scatter.3.cloned.1.call-update
  47.1 0.0 all-reduce.3.cloned.1.call-start
  47.2 27.7 %reduce-scatter.3.cloned.1.call-done = f32[64,1024]{1,0:T(8,128)} async-done(((f32[64,4096]{1,0:T(8,128)}), f32[64,1024]{1,0:T(8,128)}) %reduce-scatter.3.cloned.1.call-update) | async-done | bytes 262160 | tf_op jit(solution)/shard_map/reduce_scatter | solution.py:87
  74.9 0.0 all-reduce.3.cloned.1.call-update
  74.9 0.0 reduce-scatter.5.cloned.1.call-start
  74.9 0.4 fusion.10
  75.3 39.6 %psum.43 = f32[64,64]{1,0:T(8,128)S(1)} all-reduce(f32[64,64]{1,0:T(8,128)S(1)} %fusion.10), channel_id=1, replica_groups=mesh['pix'=8,'feat'=4] {'pix','feat'}, use_global_device_ids=true, to_apply=%region_2.0 | all-reduce | flops 4096 | bytes 32768 | tf_op jit(solution)/shard_map/psum | solution.py:89
  114.9 34.3 %all-reduce.3.cloned.1.call-done = f32[64,1024]{1,0:T(8,128)} async-done(((f32[64,1024]{1,0:T(8,128)}), f32[64,1024]{1,0:T(8,128)}) %all-reduce.3.cloned.1.call-update) | async-done | bytes 262160 | tf_op jit(solution)/shard_map/psum | solution.py:88
  149.3 0.0 copy-done.2
  149.3 1.3 fusion.8
  150.6 7.2 %all_gather.6 = bf16[64,4096]{1,0:T(8,128)(2,1)S(1)} all-gather(bf16[64,1024]{1,0:T(8,128)(2,1)S(1)} %get-tuple-element.2), channel_id=1, replica_groups=mesh['pix'=8,'feat'=4] {'feat'}, dimensions={1}, use_global_device_ids=true | all-gather | bytes 655360 | tf_op jit(solution)/shard_map/all_gather | solution.py:100
  157.8 6.0 %convolution_multiply_fusion.1 = f32[1024,64]{0,1:T(8,128)S(1)} fusion(f32[1024,64]{0,1:T(8,128)S(1)} %copy-done, bf16[1024,4096]{1,0:T(8,128)(2,1)} %shard_map.68, bf16[64,4096]{1,0:T(8,128)(2,1)S(1)} %all_gather.6), kind=kOutput, calls=%fused_computation.11 | convolution fusion | flops 536936448 | bytes 9437184 | tf_op jit(solution)/shard_map/dot_general | solution.py:98
  163.8 0.4 fusion.11
  164.2 10.9 %psum.44 = f32[64,64]{1,0:T(8,128)S(1)} all-reduce(f32[64,64]{1,0:T(8,128)S(1)} %fusion.11), channel_id=1, replica_groups=mesh['pix'=8,'feat'=4] {'feat'}, use_global_device_ids=true, to_apply=%region_3.0 | all-reduce | flops 4096 | bytes 32768 | tf_op jit(solution)/shard_map/psum | solution.py:111
  175.1 0.4 fusion.3
  175.6 6.0 %fusion.5 = f32[64,4096]{1,0:T(8,128)} fusion(bf16[1024,4096]{1,0:T(8,128)(2,1)} %shard_map.68, f32[1024,64]{0,1:T(8,128)S(1)} %fusion.3), kind=kOutput, calls=%fused_computation.12 | convolution fusion | flops 536936448 | bytes 9699328 | tf_op jit(solution)/shard_map/dot_general | solution.py:74
  181.6 0.0 reduce-scatter.5.cloned.1.call-update
  181.6 0.0 all-reduce.5.cloned.1.call-start
  181.7 24.0 %reduce-scatter.5.cloned.1.call-done = f32[64,1024]{1,0:T(8,128)} async-done(((f32[64,4096]{1,0:T(8,128)}), f32[64,1024]{1,0:T(8,128)}) %reduce-scatter.5.cloned.1.call-update) | async-done | bytes 262160 | tf_op jit(solution)/shard_map/reduce_scatter | solution.py:87
  205.6 0.0 all-reduce.5.cloned.1.call-update
  205.7 0.4 fusion.12
  206.0 39.6 %psum.46 = f32[64,64]{1,0:T(8,128)S(1)} all-reduce(f32[64,64]{1,0:T(8,128)S(1)} %fusion.12), channel_id=1, replica_groups=mesh['pix'=8,'feat'=4] {'pix','feat'}, use_global_device_ids=true, to_apply=%region_6.0 | all-reduce | flops 4096 | bytes 32768 | tf_op jit(solution)/shard_map/psum | solution.py:89
  245.6 34.4 %all-reduce.5.cloned.1.call-done = f32[64,1024]{1,0:T(8,128)} async-done(((f32[64,1024]{1,0:T(8,128)}), f32[64,1024]{1,0:T(8,128)}) %all-reduce.5.cloned.1.call-update) | async-done | bytes 262160 | tf_op jit(solution)/shard_map/psum | solution.py:88
  280.0 1.3 fusion.9
  281.3 0.0 copy-start.1
  281.3 7.1 %all_gather.7 = bf16[64,4096]{1,0:T(8,128)(2,1)S(1)} all-gather(bf16[64,1024]{1,0:T(8,128)(2,1)S(1)} %get-tuple-element.4), channel_id=1, replica_groups=mesh['pix'=8,'feat'=4] {'feat'}, dimensions={1}, use_global_device_ids=true | all-gather | bytes 655360 | tf_op jit(solution)/shard_map/all_gather | solution.py:100
  288.5 6.0 %convolution_multiply_fusion = f32[1024,64]{0,1:T(8,128)S(1)} fusion(f32[1024,64]{0,1:T(8,128)S(1)} %fusion.3, bf16[1024,4096]{1,0:T(8,128)(2,1)} %shard_map.68, bf16[64,4096]{1,0:T(8,128)(2,1)S(1)} %all_gather.7), kind=kOutput, calls=%fused_computation.10 | convolution fusion | flops 536936448 | bytes 9437184 | tf_op jit(solution)/shard_map/dot_general | solution.py:98
  294.5 0.4 fusion.13
  294.9 10.9 %psum.47 = f32[64,64]{1,0:T(8,128)S(1)} all-reduce(f32[64,64]{1,0:T(8,128)S(1)} %fusion.13), channel_id=1, replica_groups=mesh['pix'=8,'feat'=4] {'feat'}, use_global_device_ids=true, to_apply=%region_7.0 | all-reduce | flops 4096 | bytes 32768 | tf_op jit(solution)/shard_map/psum | solution.py:111
  305.8 1.1 fusion
  307.0 0.0 copy-done.1
Async XLA Ops:
  7.2 33.9 %copy-start = (f32[1024,64]{0,1:T(8,128)S(1)}, f32[1024,64]{0,1:T(8,128)}, u32[]{:S(2)}) copy-start(f32[1024,64]{0,1:T(8,128)} %param.8) | copy-start | bytes 786436
  7.2 67.7 %reduce-scatter.3.cloned.1.call-start = ((), (), s32[]{:S(2)}) async-start(), calls=%async_computation.2 | async-start | bytes 1310720 | tf_op jit(solution)/shard_map/reduce_scatter | solution.py:87
  41.0 108.2 %copy-start.2 = (f32[64,1024]{1,0:T(8,128)S(1)}, f32[64,1024]{1,0:T(8,128)}, u32[]{:S(2)}) copy-start(f32[64,1024]{1,0:T(8,128)} %param.9) | copy-start | bytes 786436
  47.1 102.1 %all-reduce.3.cloned.1.call-start = ((), (), s32[]{:S(2)}) async-start(), calls=%async_computation.3 | async-start | bytes 524288 | tf_op jit(solution)/shard_map/psum | solution.py:88
  74.9 130.8 %reduce-scatter.5.cloned.1.call-start = ((), (), s32[]{:S(2)}) async-start(), calls=%async_computation.4 | async-start | bytes 1310720 | tf_op jit(solution)/shard_map/reduce_scatter | solution.py:87
  181.6 98.4 %all-reduce.5.cloned.1.call-start = ((), (), s32[]{:S(2)}) async-start(), calls=%async_computation.5 | async-start | bytes 524288 | tf_op jit(solution)/shard_map/psum | solution.py:88
  281.3 25.6 %copy-start.1 = (f32[64,1024]{1,0:T(8,128)}, f32[64,1024]{1,0:T(8,128)S(1)}, u32[]{:S(2)}) copy-start(f32[64,1024]{1,0:T(8,128)S(1)} %get-tuple-element.5) | copy-start | bytes 786436
Sparse Core Ops, SparseCore 0:
  47.2 27.5 reduce-scatter.2
  78.6 70.6 all-reduce.2
  181.7 23.8 reduce-scatter.4
  209.2 70.7 all-reduce.4

commit v2 on v1

--- a/solution.py
+++ b/solution.py
@@ -1,3 +1,5 @@
+import functools
+
 import jax
 import jax.numpy as jnp
 from jax import lax
@@ -66,58 +68,219 @@
     )(mass, mobility, weight)
 
 
-def local(mass_bin, mobility_bin, intensity, basis_init, profile_init):
-    spectra = bin_peaks(mass_bin, mobility_bin, intensity)
+def nmf_kernel(
+    pixes, chips, spectra_ref, basis_in, profiles_in, basis_ref, profiles_ref,
+    pair_out, pair_in, gram_out, gram_in, chip_out, chip_in, pix_out, pix_in, whole_ref,
+    rounded_ref, gram_h_out, gram_h_in, gram_h_pair_out, gram_h_pair_in, padded_ref,
+    pair_sem, gram_sem, chip_sem, pix_sem, whole_sem, block_sem, block_pair_sem, gram_h_sem, gram_h_pair_sem,
+):
+    rank, width = profiles_in.shape
+    share = rank // pixes
+    pix, feat = lax.axis_index("pix"), lax.axis_index("feat")
+    core, chip = lax.rem(feat, 2), feat // 2
+    other = 1 - core
+    partner = (pix, chip * 2 + other)
     highest = lax.Precision.HIGHEST
-    basis, profiles = (basis_init, profile_init)
+
+    def chip_at(j):
+        return lax.rem(chip + j + chips, chips)
+
+    def pix_at(d):
+        return lax.rem(pix + d + pixes, pixes)
+
+    barrier = pltpu.get_barrier_semaphore()
+    peers = [partner] + [(pix, chip_at(j) * 2 + core) for j in range(1, chips)]
+    peers += [(pix_at(d), feat) for d in range(1, pixes)]
+    for peer in peers:
+        pl.semaphore_signal(barrier, inc=1, device_id=peer, device_id_type=pl.DeviceIdType.MESH)
+    pl.semaphore_wait(barrier, len(peers))
+
+    started = []
+
+    def send(src, dst, sems, device):
+        copy = pltpu.make_async_remote_copy(
+            src_ref=src, dst_ref=dst, send_sem=sems.at[0], recv_sem=sems.at[1],
+            device_id=device, device_id_type=pl.DeviceIdType.MESH,
+        )
+        copy.start()
+        started.append(copy)
+        return copy
+
+    def columns(block):
+        return pl.ds(pl.multiple_of(block * width, LANES), width)
+
+    padded_ref[...] = jnp.zeros_like(padded_ref)
+    gram_h_out[...] = jnp.zeros_like(gram_h_out)
+    basis, profiles = basis_in[...], profiles_in[...]
     for step in range(ITERS):
-        partial_h = lax.dot_general(
-            basis.astype(jnp.bfloat16),
-            spectra,
-            (((0,), (0,)), ((), ())),
-            preferred_element_type=jnp.float32,
-        )
-        partial_gram = lax.dot_general(
-            basis,
-            basis,
-            (((0,), (0,)), ((), ())),
-            precision=highest,
-            preferred_element_type=jnp.float32,
-        )
-        shared = lax.psum_scatter(partial_h, "feat", scatter_dimension=1, tiled=True)
-        numer_h = lax.psum(shared, "pix")
-        gram_w = lax.psum(partial_gram, ("pix", "feat"))
+        padded_ref[:, :rank] = basis
+        padded = padded_ref[...]
+        turned = padded.T[:rank, :]
+        turned_b = turned.astype(jnp.bfloat16)
+
+        def numer(block):
+            return jnp.dot(
+                turned_b, spectra_ref[:, columns(block)], preferred_element_type=jnp.float32
+            )
+
+        order = list(range(1, chips)) + [0]
+        pair = {}
+        for j in order:
+            pair_out[step, j] = numer(chip_at(j) * 2 + other)
+            pair[j] = send(pair_out.at[step, j], pair_in.at[step, j], pair_sem.at[step, j], partner)
+        gram_out[step] = jnp.dot(turned, padded, precision=highest, preferred_element_type=jnp.float32)
+        gram_copy = send(gram_out.at[step], gram_in.at[step], gram_sem.at[step], partner)
+        chip_copy = {}
+        for j in order:
+            mine = numer(chip_at(j) * 2 + core)
+            if j == order[0]:
+                gram_copy.wait_recv()
+                gram = gram_out[step] + gram_in[step]
+            pair[j].wait_recv()
+            chip_out[step, j, :, :width] = mine + pair_in[step, j]
+            chip_out[step, j, :, width:] = gram
+            if j:
+                chip_copy[j] = send(
+                    chip_out.at[step, j], chip_in.at[step, j], chip_sem.at[step, j], (pix, chip_at(j) * 2 + core)
+                )
+        total = chip_out[step, 0]
+        for j in range(1, chips):
+            chip_copy[j].wait_recv()
+            total = total + chip_in[step, j]
+        if share % 8 == 0:
+            pix_out[step] = total.reshape(pixes, share, width + LANES)
+        else:
+            for d in range(pixes):
+                pix_out[step, d] = total[d * share : (d + 1) * share]
+        copies = [
+            send(pix_out.at[step, pix_at(d)], pix_in.at[step, d], pix_sem.at[step, d], (pix_at(d), feat))
+            for d in range(1, pixes)
+        ]
+        part = pix_out[step, pix]
+        for d in range(1, pixes):
+            copies[d - 1].wait_recv()
+            part = part + pix_in[step, d]
+        whole_ref[step, pix] = part
+        copies = [
+            send(whole_ref.at[step, pix], whole_ref.at[step, pix], whole_sem.at[step, d], (pix_at(d), feat))
+            for d in range(1, pixes)
+        ]
+        for copy in copies:
+            copy.wait_recv()
+        if share % 8 == 0:
+            whole = whole_ref[step].reshape(rank, width + LANES)
+        else:
+            for d in range(pixes):
+                chip_out[step, 0, d * share : (d + 1) * share] = whole_ref[step, d]
+            whole = chip_out[step, 0]
+        gram_w = whole[:, width : width + rank]
         profiles = (
             profiles
-            * numer_h
-            / (
-                jnp.dot(gram_w, profiles, precision=highest, preferred_element_type=jnp.float32)
-                + EPS
-            )
-        )
-        numer_w = lax.dot_general(
-            spectra,
-            lax.all_gather(profiles.astype(jnp.bfloat16), "feat", axis=1, tiled=True),
-            (((1,), (1,)), ((), ())),
-            preferred_element_type=jnp.float32,
-        )
-        local_gram = lax.dot_general(
-            profiles,
-            profiles,
-            (((1,), (1,)), ((), ())),
-            precision=highest,
-            preferred_element_type=jnp.float32,
-        )
-        gram_h = lax.psum(local_gram, "feat")
+            * whole[:, :width]
+            / (jnp.dot(gram_w, profiles, precision=highest, preferred_element_type=jnp.float32) + EPS)
+        )
+        rounded_ref[step, feat] = profiles.astype(jnp.bfloat16)
+        mine = rounded_ref.at[step, feat]
+        block_copy = {
+            j: send(mine, mine, block_sem.at[step, j], (pix, chip_at(j) * 2 + core)) for j in range(1, chips)
+        }
+        block_pair = {0: send(mine, mine, block_pair_sem.at[step, 0], partner)}
+        gram_h_out[step, :, :rank] = lax.dot_general(
+            profiles, profiles, (((1,), (1,)), ((), ())), precision=highest, preferred_element_type=jnp.float32
+        )
+        gram_h_copy = {
+            j: send(gram_h_out.at[step], gram_h_in.at[step, j], gram_h_sem.at[step, j], (pix, chip_at(j) * 2 + core))
+            for j in range(1, chips)
+        }
+
+        def weigh(block):
+            return lax.dot_general(
+                spectra_ref[:, columns(block)],
+                rounded_ref[step, block],
+                (((1,), (1,)), ((), ())),
+                preferred_element_type=jnp.float32,
+            )
+
+        numer_w = weigh(feat)
+        gram_h = gram_h_out[step]
+        for j in range(1, chips):
+            block_copy[j].wait_recv()
+            came = rounded_ref.at[step, chip_at(-j) * 2 + core]
+            block_pair[j] = send(came, came, block_pair_sem.at[step, j], partner)
+            gram_h_copy[j].wait_recv()
+            gram_h = gram_h + gram_h_in[step, j]
+        gram_h_pair_out[step] = gram_h
+        gram_h_pair = send(
+            gram_h_pair_out.at[step], gram_h_pair_in.at[step], gram_h_pair_sem.at[step], partner
+        )
+        for j in range(1, chips):
+            numer_w = numer_w + weigh(chip_at(-j) * 2 + core)
+        for j in range(chips):
+            block_pair[j].wait_recv()
+            numer_w = numer_w + weigh(chip_at(-j) * 2 + other)
+        gram_h_pair.wait_recv()
+        gram_h = (gram_h + gram_h_pair_in[step])[:, :rank]
         basis = (
             basis
             * numer_w
             / (jnp.dot(basis, gram_h, precision=highest, preferred_element_type=jnp.float32) + EPS)
         )
-    return (basis, profiles)
+    basis_ref[...] = basis
+    profiles_ref[...] = profiles
+    for copy in started:
+        copy.wait_send()
+
+
+def nmf(pixes, feats, spectra, basis, profiles):
+    rank, width = profiles.shape
+    rows = basis.shape[0]
+    chips, share = feats // 2, rank // pixes
+    f32 = jnp.float32
+    dma = pltpu.SemaphoreType.DMA
+    return pl.pallas_call(
+        functools.partial(nmf_kernel, pixes, chips),
+        out_shape=[jax.ShapeDtypeStruct(basis.shape, f32), jax.ShapeDtypeStruct(profiles.shape, f32)],
+        in_specs=[pl.BlockSpec(memory_space=pltpu.VMEM)] * 3,
+        out_specs=[pl.BlockSpec(memory_space=pltpu.VMEM)] * 2,
+        scratch_shapes=[
+            pltpu.VMEM((ITERS, chips, rank, width), f32),
+            pltpu.VMEM((ITERS, chips, rank, width), f32),
+            pltpu.VMEM((ITERS, rank, LANES), f32),
+            pltpu.VMEM((ITERS, rank, LANES), f32),
+            pltpu.VMEM((ITERS, chips, rank, width + LANES), f32),
+            pltpu.VMEM((ITERS, chips, rank, width + LANES), f32),
+            pltpu.VMEM((ITERS, pixes, share, width + LANES), f32),
+            pltpu.VMEM((ITERS, pixes, share, width + LANES), f32),
+            pltpu.VMEM((ITERS, pixes, share, width + LANES), f32),
+            pltpu.VMEM((ITERS, feats, rank, width), jnp.bfloat16),
+            pltpu.VMEM((ITERS, rank, LANES), f32),
+            pltpu.VMEM((ITERS, chips, rank, LANES), f32),
+            pltpu.VMEM((ITERS, rank, LANES), f32),
+            pltpu.VMEM((ITERS, rank, LANES), f32),
+            pltpu.VMEM((rows, LANES), f32),
+            dma((ITERS, chips, 2)),
+            dma((ITERS, 2)),
+            dma((ITERS, chips, 2)),
+            dma((ITERS, pixes, 2)),
+            dma((ITERS, pixes, 2)),
+            dma((ITERS, chips, 2)),
+            dma((ITERS, chips, 2)),
+            dma((ITERS, chips, 2)),
+            dma((ITERS, 2)),
+        ],
+        compiler_params=pltpu.CompilerParams(
+            collective_id=0, has_side_effects=True, vmem_limit_bytes=44 * 1024 * 1024
+        ),
+    )(spectra, basis, profiles)
 
 
 def solution(mesh):
+    pixes, feats = mesh.shape["pix"], mesh.shape["feat"]
+
+    def local(mass_bin, mobility_bin, intensity, basis_init, profile_init):
+        spectra = bin_peaks(mass_bin, mobility_bin, intensity)
+        return tuple(nmf(pixes, feats, spectra, basis_init, profile_init))
+
     return jax.shard_map(
         local,
         mesh=mesh,

time: 314 us -> 121 us (0.39)
  waiting for transfers between devices: 120 us -> 0 us
  blocking collectives: 115 us -> 0 us
  Pallas kernels: 33.8 us -> 114 us
  matrix products: 29.8 us -> 0 us
  between operations: 13.9 us -> 0.66 us
  local copies, waits for them, and re-layouts: 0.01 us -> 6.16 us
    psum x4 -> x0, blocking collectives: 101 us -> none  [the longest x2 79.2 us: local(): gram_w = lax.psum(partial_gram, ('pix', 'feat'))]
    pallas_call x0 -> x1, Pallas kernels: none -> 80.5 us  [nmf(): pl.pallas_call(functools.partial(nmf_kernel, pixes, chips), out_shape=[ja...]
    psum x2 -> x0, waiting for transfers between devices: 68.7 us -> none  [local(): numer_h = lax.psum(shared, 'pix')]
    reduce_scatter x2 -> x0, waiting for transfers between devices: 51.7 us -> none  [local(): lax.psum_scatter(partial_h, 'feat', scatter_dimension=1, tiled=True)]
    dot_general x12 -> x0, matrix products: 29.8 us -> none  [the longest x2 12.1 us: local(): lax.dot_general(basis.astype(jnp.bfloat16), spectra, (((0,), (0,)), ((),...]
    all_gather x2 -> x0, blocking collectives: 14.3 us -> none  [local(): lax.all_gather(profiles.astype(jnp.bfloat16), 'feat', axis=1, tiled=True)]
    unnamed x6, local copies, waits for them, and re-layouts: 0.01 us -> 5.27 us
  transfers between devices with their start and end apart: 4 -> 0, of which waited for: 4 -> 0; matrix products, arithmetic and copies ran while one was open for 0% -> 0% of each run, Pallas kernels for 0% -> 0%
where the time goes in v2:
time: 121 us
  Pallas kernels  114 us (94%)
  local copies, waits for them, and re-layouts  6.16 us (5%)
    pallas_call x1, Pallas kernels, nmf(): pl.pallas_call(functools.partial(nmf_kernel, pixes, chips), out_shape=[ja...  80.5 us
    pallas_call x1, Pallas kernels, bin_peaks(): pl.pallas_call(bin_kernel, out_shape=jax.ShapeDtypeStruct((rows, MZ * MOB...  33.8 us
    unnamed x6, local copies, waits for them, and re-layouts  5.27 us

profile of v2, /device:TPU:0, one launch (start us, length us, event | category | flops | bytes accessed | tf_op | source)
XLA Modules:
  0.0 121.2 jit_solution(14932919943175753332)
XLA Ops:
  0.6 0.0 copy-start.1
  0.6 1.2 copy.7.basis_in
  1.8 33.8 %shard_map.68.spectra_ref = bf16[1024,4096]{1,0:T(8,128)(2,1)} custom-call(s32[1024,256]{1,0:T(8,128)} %mass_ref.1, s32[1024,256]{1,0:T(8,128)} %mobility_ref.1, bf16[1024,256]{1,0:T(8,128)(2,1)} %weight_ref.1), custom_call_target="tpu_custom_call" | custom-call | flops 2147483648 | bytes 11010048 | tf_op jit(solution)/shard_map/pallas_call | solution.py:57
  35.6 0.0 copy-done.1
  35.6 0.0 copy-start
  35.6 3.4 %copy-done = bf16[1024,4096]{1,0:T(8,128)(2,1)S(1)} copy-done((bf16[1024,4096]{1,0:T(8,128)(2,1)S(1)}, bf16[1024,4096]{1,0:T(8,128)(2,1)}, u32[]{:S(2)}) %copy-start) | copy-done | bytes 8388632
  39.0 80.5 %shard_map.69 = (f32[1024,64]{1,0:T(8,128)S(1)}, f32[64,1024]{1,0:T(8,128)S(1)}) custom-call(bf16[1024,4096]{1,0:T(8,128)(2,1)S(1)} %copy-done, f32[1024,64]{1,0:T(8,128)S(1)} %copy.7.basis_in, f32[64,1024]{1,0:T(8,128)S(1)} %copy-done.1), custom_call_target="tpu_custom_call" | custom-call | tf_op jit(solution)/shard_map/pallas_call | solution.py:240
  119.6 0.9 copy.8
  120.5 0.7 copy.10
Async XLA Ops:
  0.6 35.0 %copy-start.1 = (f32[64,1024]{1,0:T(8,128)S(1)}, f32[64,1024]{1,0:T(8,128)}, u32[]{:S(2)}) copy-start(f32[64,1024]{1,0:T(8,128)} %profiles_in.1) | copy-start | bytes 786436
  35.6 3.4 %copy-start = (bf16[1024,4096]{1,0:T(8,128)(2,1)S(1)}, bf16[1024,4096]{1,0:T(8,128)(2,1)}, u32[]{:S(2)}) copy-start(bf16[1024,4096]{1,0:T(8,128)(2,1)} %shard_map.68.spectra_ref) | copy-start | bytes 25165828

commit v3 on v2

v3 whole, which is shorter than its diff:
```python
import functools

import jax
import jax.numpy as jnp
from jax import lax
from jax.experimental import pallas as pl
from jax.experimental.pallas import tpu as pltpu
from jax.sharding import PartitionSpec as P

LANES = 128
MZ = 256
MOB = 16
HI = MZ * MOB // LANES
GROUP = 16
ITERS = 2
HALVES = 2
EPS = 1e-06


def bin_kernel(mass_ref, mobility_ref, weight_ref, out_ref, hi_ref, lo_ref, value_ref, dense_ref):
    rows, peaks = mass_ref.shape
    mass = mass_ref[...]
    hi_ref[...] = (mobility_ref[...] * (MZ // LANES) + mass // LANES).astype(jnp.float32)
    lo_ref[...] = (mass % LANES).astype(jnp.float32)
    value_ref[...] = weight_ref[...].astype(jnp.float32)
    hi_iota = lax.broadcasted_iota(jnp.int32, (HI, peaks), 0).astype(jnp.float32).astype(jnp.bfloat16)
    lo_iota = lax.broadcasted_iota(jnp.int32, (LANES, peaks), 0).astype(jnp.float32).astype(jnp.bfloat16)

    def spread(ref, p, count):
        return jnp.broadcast_to(ref[pl.ds(p, 1), :], (count, peaks)).astype(jnp.bfloat16)

    def group(g, _):
        base = pl.multiple_of(g * GROUP, GROUP)
        for i in range(GROUP):
            p = base + i
            left = jnp.where(
                spread(hi_ref, p, HI) == hi_iota, spread(value_ref, p, HI), jnp.bfloat16(0)
            )
            right = jnp.where(
                spread(lo_ref, p, LANES) == lo_iota, jnp.bfloat16(1), jnp.bfloat16(0)
            )
            dense_ref[pl.ds(i, HI, stride=GROUP), :] = lax.dot_general(
                left, right, (((1,), (1,)), ((), ())), preferred_element_type=jnp.float32
            )
        for h in range(HI):
            out_ref[pl.ds(base, GROUP), h * LANES : (h + 1) * LANES] = dense_ref[
                h * GROUP : (h + 1) * GROUP, :
            ].astype(jnp.bfloat16)
        return 0

    lax.fori_loop(0, rows // GROUP, group, 0)


def bin_peaks(mass, mobility, weight):
    rows, peaks = mass.shape
    block = 128
    spec = pl.BlockSpec((block, peaks), lambda i: (i, 0))
    return pl.pallas_call(
        bin_kernel,
        out_shape=jax.ShapeDtypeStruct((rows, MZ * MOB), jnp.bfloat16),
        grid=(rows // block,),
        in_specs=[spec] * 3,
        out_specs=pl.BlockSpec((block, MZ * MOB), lambda i: (i, 0)),
        scratch_shapes=[pltpu.VMEM((block, peaks), jnp.float32)] * 3
        + [pltpu.VMEM((HI * GROUP, LANES), jnp.float32)],
        cost_estimate=pl.CostEstimate(
            flops=2 * rows * peaks * MZ * MOB, bytes_accessed=rows * (peaks * 10 + MZ * MOB * 2), transcendentals=0
        ),
    )(mass, mobility, weight)


def nmf_kernel(
    pixes, chips, spectra_ref, basis_in, profiles_in, basis_ref, profiles_ref,
    pair_out, pair_in, gram_out, gram_in, chip_out, chip_in, pix_out, pix_in, whole_ref,
    rounded_ref, gram_h_out, gram_h_in, gram_h_pair_out, gram_h_pair_in, padded_ref,
    pair_sem, gram_sem, chip_sem, pix_sem, whole_sem, block_sem, block_pair_sem, gram_h_sem, gram_h_pair_sem,
):
    rank, width = profiles_in.shape
    span = width // HALVES
    share = rank // pixes
    pix, feat = lax.axis_index("pix"), lax.axis_index("feat")
    core, chip = lax.rem(feat, 2), feat // 2
    other = 1 - core
    partner = (pix, chip * 2 + other)
    highest = lax.Precision.HIGHEST

    def chip_at(j):
        return lax.rem(chip + j + chips, chips)

    def pix_at(d):
        return lax.rem(pix + d + pixes, pixes)

    barrier = pltpu.get_barrier_semaphore()
    peers = [partner] + [(pix, chip_at(j) * 2 + core) for j in range(1, chips)]
    peers += [(pix_at(d), feat) for d in range(1, pixes)]
    for peer in peers:
        pl.semaphore_signal(barrier, inc=1, device_id=peer, device_id_type=pl.DeviceIdType.MESH)
    pl.semaphore_wait(barrier, len(peers))

    started = []

    def send(src, dst, sems, device):
        copy = pltpu.make_async_remote_copy(
            src_ref=src, dst_ref=dst, send_sem=sems.at[0], recv_sem=sems.at[1],
            device_id=device, device_id_type=pl.DeviceIdType.MESH,
        )
        copy.start()
        started.append(copy)
        return copy

    def columns(block, half):
        return pl.ds(pl.multiple_of(block * width + half * span, LANES), span)

    def reach(half):
        return pl.ds(0, span if half else span + LANES)

    gram_out[...] = jnp.zeros_like(gram_out)
    gram_h_out[...] = jnp.zeros_like(gram_h_out)
    padded_ref[...] = jnp.zeros_like(padded_ref)
    basis = basis_in[...]
    profiles = [profiles_in[:, half * span : (half + 1) * span] for half in range(HALVES)]
    order = list(range(1, chips)) + [0]
    nt = (((1,), (1,)), ((), ()))
    for step in range(ITERS):
        basis_b = basis.astype(jnp.bfloat16)

        def numer(block, half):
            return jnp.dot(
                basis_b, spectra_ref[:, columns(block, half)], preferred_element_type=jnp.float32
            )

        pair, chip_copy, pix_copy, whole_copy, block_copy, block_pair = {}, {}, {}, {}, {}, {}
        for half in range(HALVES):
            for j in order:
                pair_out[step, half, j] = numer(chip_at(j) * 2 + other, half)
                pair[half, j] = send(
                    pair_out.at[step, half, j], pair_in.at[step, half, j], pair_sem.at[step, half, j], partner
                )
            if half == 0:
                gram_out[step, :, :rank] = lax.dot_general(
                    basis, basis, nt, precision=highest, preferred_element_type=jnp.float32
                )
                gram_copy = send(gram_out.at[step], gram_in.at[step], gram_sem.at[step], partner)
            for j in order:
                mine = numer(chip_at(j) * 2 + core, half)
                if half == 0 and j == order[0]:
                    gram_copy.wait_recv()
                    gram = gram_out[step] + gram_in[step]
                pair[half, j].wait_recv()
                chip_out[step, half, j, :, :span] = mine + pair_in[step, half, j]
                if half == 0:
                    chip_out[step, half, j, :, span:] = gram
                if j:
                    chip_copy[half, j] = send(
                        chip_out.at[step, half, j, :, reach(half)],
                        chip_in.at[step, half, j, :, reach(half)],
                        chip_sem.at[step, half, j],
                        (pix, chip_at(j) * 2 + core),
                    )
        for half in range(HALVES):
            size = span if half else span + LANES
            total = chip_out[step, half, 0, :, :size]
            for j in range(1, chips):
                chip_copy[half, j].wait_recv()
                total = total + chip_in[step, half, j, :, :size]
            if share % 8 == 0:
                pix_out[step, half, :, :, :size] = total.reshape(pixes, share, size)
            else:
                for d in range(pixes):
                    pix_out[step, half, d, :, :size] = total[d * share : (d + 1) * share]
            for d in range(1, pixes):
                pix_copy[half, d] = send(
                    pix_out.at[step, half, pix_at(d), :, reach(half)],
                    pix_in.at[step, half, d, :, reach(half)],
                    pix_sem.at[step, half, d],
                    (pix_at(d), feat),
                )
        for half in range(HALVES):
            size = span if half else span + LANES
            part = pix_out[step, half, pix, :, :size]
            for d in range(1, pixes):
                pix_copy[half, d].wait_recv()
                part = part + pix_in[step, half, d, :, :size]
            whole_ref[step, half, pix, :, :size] = part
            for d in range(1, pixes):
                own = whole_ref.at[step, half, pix, :, reach(half)]
                whole_copy[half, d] = send(own, own, whole_sem.at[step, half, d], (pix_at(d), feat))
        for half in range(HALVES):
            size = span if half else span + LANES
            for d in range(1, pixes):
                whole_copy[half, d].wait_recv()
            if share % 8 == 0:
                whole = whole_ref[step, half, :, :, :size].reshape(rank, size)
            else:
                for d in range(pixes):
                    chip_out[step, half, 0, d * share : (d + 1) * share, :size] = whole_ref[step, half, d, :, :size]
                whole = chip_out[step, half, 0, :, :size]
            if half == 0:
                gram_w = whole[:, span : span + rank]
            profiles[half] = (
                profiles[half]
                * whole[:, :span]
                / (jnp.dot(gram_w, profiles[half], precision=highest, preferred_element_type=jnp.float32) + EPS)
            )
            rounded_ref[step, half, feat] = profiles[half].astype(jnp.bfloat16)
            mine = rounded_ref.at[step, half, feat]
            for j in range(1, chips):
                block_copy[half, j] = send(
                    mine, mine, block_sem.at[step, half, j], (pix, chip_at(j) * 2 + core)
                )
            block_pair[half, 0] = send(mine, mine, block_pair_sem.at[step, half, 0], partner)
            part = lax.dot_general(
                profiles[half], profiles[half], nt, precision=highest, preferred_element_type=jnp.float32
            )
            gram_h = gram_h + part if half else part
        gram_h_out[step, :, :rank] = gram_h
        gram_h_copy = {
            j: send(gram_h_out.at[step], gram_h_in.at[step, j], gram_h_sem.at[step, j], (pix, chip_at(j) * 2 + core))
            for j in range(1, chips)
        }

        def weigh(block, half):
            return lax.dot_general(
                spectra_ref[:, columns(block, half)],
                rounded_ref[step, half, block],
                nt,
                preferred_element_type=jnp.float32,
            )

        numer_w = weigh(feat, 0)
        for half in range(1, HALVES):
            numer_w = numer_w + weigh(feat, half)
        for half in range(HALVES):
            block_pair[half, 0].wait_recv()
            numer_w = numer_w + weigh(chip * 2 + other, half)
        for half in range(HALVES):
            for j in range(1, chips):
                block_copy[half, j].wait_recv()
                came = rounded_ref.at[step, half, chip_at(-j) * 2 + core]
                block_pair[half, j] = send(came, came, block_pair_sem.at[step, half, j], partner)
                numer_w = numer_w + weigh(chip_at(-j) * 2 + core, half)
        gram_h = gram_h_out[step]
        for j in range(1, chips):
            gram_h_copy[j].wait_recv()
            gram_h = gram_h + gram_h_in[step, j]
        gram_h_pair_out[step] = gram_h
        gram_h_pair = send(
            gram_h_pair_out.at[step], gram_h_pair_in.at[step], gram_h_pair_sem.at[step], partner
        )
        for half in range(HALVES):
            for j in range(1, chips):
                block_pair[half, j].wait_recv()
                numer_w = numer_w + weigh(chip_at(-j) * 2 + other, half)
        gram_h_pair.wait_recv()
        gram_h = (gram_h + gram_h_pair_in[step])[:, :rank]
        padded_ref[:, :rank] = numer_w
        basis = (
            basis
            * padded_ref[...].T[:rank, :]
            / (jnp.dot(gram_h, basis, precision=highest, preferred_element_type=jnp.float32) + EPS)
        )
    basis_ref[...] = basis
    for half in range(HALVES):
        profiles_ref[:, half * span : (half + 1) * span] = profiles[half]
    for copy in started:
        copy.wait_send()


def nmf(pixes, feats, spectra, basis, profiles):
    rank, width = profiles.shape
    rows, span = basis.shape[1], width // HALVES
    chips, share = feats // 2, rank // pixes
    f32 = jnp.float32
    dma = pltpu.SemaphoreType.DMA
    return pl.pallas_call(
        functools.partial(nmf_kernel, pixes, chips),
        out_shape=[jax.ShapeDtypeStruct(basis.shape, f32), jax.ShapeDtypeStruct(profiles.shape, f32)],
        in_specs=[pl.BlockSpec(memory_space=pltpu.VMEM)] * 3,
        out_specs=[pl.BlockSpec(memory_space=pltpu.VMEM)] * 2,
        scratch_shapes=[
            pltpu.VMEM((ITERS, HALVES, chips, rank, span), f32),
            pltpu.VMEM((ITERS, HALVES, chips, rank, span), f32),
            pltpu.VMEM((ITERS, rank, LANES), f32),
            pltpu.VMEM((ITERS, rank, LANES), f32),
            pltpu.VMEM((ITERS, HALVES, chips, rank, span + LANES), f32),
            pltpu.VMEM((ITERS, HALVES, chips, rank, span + LANES), f32),
            pltpu.VMEM((ITERS, HALVES, pixes, share, span + LANES), f32),
            pltpu.VMEM((ITERS, HALVES, pixes, share, span + LANES), f32),
            pltpu.VMEM((ITERS, HALVES, pixes, share, span + LANES), f32),
            pltpu.VMEM((ITERS, HALVES, feats, rank, span), jnp.bfloat16),
            pltpu.VMEM((ITERS, rank, LANES), f32),
            pltpu.VMEM((ITERS, chips, rank, LANES), f32),
            pltpu.VMEM((ITERS, rank, LANES), f32),
            pltpu.VMEM((ITERS, rank, LANES), f32),
            pltpu.VMEM((rows, LANES), f32),
            dma((ITERS, HALVES, chips, 2)),
            dma((ITERS, 2)),
            dma((ITERS, HALVES, chips, 2)),
            dma((ITERS, HALVES, pixes, 2)),
            dma((ITERS, HALVES, pixes, 2)),
            dma((ITERS, HALVES, chips, 2)),
            dma((ITERS, HALVES, chips, 2)),
            dma((ITERS, chips, 2)),
            dma((ITERS, 2)),
        ],
        compiler_params=pltpu.CompilerParams(
            collective_id=0, has_side_effects=True, vmem_limit_bytes=44 * 1024 * 1024
        ),
    )(spectra, basis, profiles)


def solution(mesh):
    pixes, feats = mesh.shape["pix"], mesh.shape["feat"]

    def local(mass_bin, mobility_bin, intensity, basis_init, profile_init):
        spectra = bin_peaks(mass_bin, mobility_bin, intensity)
        basis, profiles = nmf(pixes, feats, spectra, basis_init.T, profile_init)
        return (basis.T, profiles)

    return jax.shard_map(
        local,
        mesh=mesh,
        in_specs=(
            P(("pix", "feat"), None),
            P(("pix", "feat"), None),
            P(("pix", "feat"), None),
            P(("pix", "feat"), None),
            P(None, "feat"),
        ),
        out_specs=(P(("pix", "feat"), None), P(None, "feat")),
        check_vma=False,
    )
```

time: 121 us -> 106 us (0.88)
  Pallas kernels: 114 us -> 101 us
  local copies, waits for them, and re-layouts: 6.16 us -> 4.79 us
    pallas_call x1, Pallas kernels: 80.5 us -> 66.9 us  [nmf(): pl.pallas_call(functools.partial(nmf_kernel, pixes, chips), out_shape=[ja...]
    unnamed x6 -> x8, local copies, waits for them, and re-layouts: 5.27 us -> 4.79 us
where the time goes in v3:
time: 106 us
  Pallas kernels  101 us (95%)
  local copies, waits for them, and re-layouts  4.79 us (5%)
    pallas_call x1, Pallas kernels, nmf(): pl.pallas_call(functools.partial(nmf_kernel, pixes, chips), out_shape=[ja...  66.9 us
    pallas_call x1, Pallas kernels, bin_peaks(): pl.pallas_call(bin_kernel, out_shape=jax.ShapeDtypeStruct((rows, MZ * MOB...  33.9 us
    unnamed x8, local copies, waits for them, and re-layouts  4.79 us

profile of v3, /device:TPU:0, one launch (start us, length us, event | category | flops | bytes accessed | tf_op | source)
XLA Modules:
  0.0 106.2 jit_solution(10881992160085507910)
XLA Ops:
  0.6 0.0 copy-start.2
  0.6 0.0 copy-start.1
  0.7 33.9 %shard_map.68.spectra_ref = bf16[1024,4096]{1,0:T(8,128)(2,1)} custom-call(s32[1024,256]{1,0:T(8,128)} %mass_ref.1, s32[1024,256]{1,0:T(8,128)} %mobility_ref.1, bf16[1024,256]{1,0:T(8,128)(2,1)} %weight_ref.1), custom_call_target="tpu_custom_call" | custom-call | flops 2147483648 | bytes 11010048 | tf_op jit(solution)/shard_map/pallas_call | solution.py:58
  34.5 0.0 copy-done.2
  34.5 0.0 copy-done.1
  34.5 0.0 copy-start
  34.5 3.4 %copy-done = bf16[1024,4096]{1,0:T(8,128)(2,1)S(1)} copy-done((bf16[1024,4096]{1,0:T(8,128)(2,1)S(1)}, bf16[1024,4096]{1,0:T(8,128)(2,1)}, u32[]{:S(2)}) %copy-start) | copy-done | bytes 8388632
  37.9 66.9 %shard_map.69 = (f32[64,1024]{1,0:T(8,128)S(1)}, f32[64,1024]{1,0:T(8,128)S(1)}) custom-call(bf16[1024,4096]{1,0:T(8,128)(2,1)S(1)} %copy-done, f32[64,1024]{1,0:T(8,128)S(1)} %bitcast.2, f32[64,1024]{1,0:T(8,128)S(1)} %copy-done.2), custom_call_target="tpu_custom_call" | custom-call | tf_op jit(solution)/shard_map/pallas_call | solution.py:275
  104.8 0.7 copy.9
  105.5 0.7 copy.10
Async XLA Ops:
  0.6 33.9 %copy-start.2 = (f32[64,1024]{1,0:T(8,128)S(1)}, f32[64,1024]{1,0:T(8,128)}, u32[]{:S(2)}) copy-start(f32[64,1024]{1,0:T(8,128)} %profiles_in.1) | copy-start | bytes 786436
  0.6 33.9 %copy-start.1 = (f32[1024,64]{0,1:T(8,128)S(1)}, f32[1024,64]{0,1:T(8,128)}, u32[]{:S(2)}) copy-start(f32[1024,64]{0,1:T(8,128)} %param.8) | copy-start | bytes 786436
  34.5 3.4 %copy-start = (bf16[1024,4096]{1,0:T(8,128)(2,1)S(1)}, bf16[1024,4096]{1,0:T(8,128)(2,1)}, u32[]{:S(2)}) copy-start(bf16[1024,4096]{1,0:T(8,128)(2,1)} %shard_map.68.spectra_ref) | copy-start | bytes 25165828

commit v4 on v3

--- a/solution.py
+++ b/solution.py
@@ -12,68 +12,73 @@
 MOB = 16
 HI = MZ * MOB // LANES
 GROUP = 16
+CHUNK = 128
 ITERS = 2
 HALVES = 2
 EPS = 1e-06
 
 
-def bin_kernel(mass_ref, mobility_ref, weight_ref, out_ref, hi_ref, lo_ref, value_ref, dense_ref):
-    rows, peaks = mass_ref.shape
-    mass = mass_ref[...]
-    hi_ref[...] = (mobility_ref[...] * (MZ // LANES) + mass // LANES).astype(jnp.float32)
-    lo_ref[...] = (mass % LANES).astype(jnp.float32)
-    value_ref[...] = weight_ref[...].astype(jnp.float32)
+def bin_peaks(mass_any, mobility_any, weight_any, out_ref, mass_ref, mobility_ref, weight_ref, hi_ref, lo_ref, value_ref, dense_ref, in_sem):
+    rows, peaks = mass_any.shape
     hi_iota = lax.broadcasted_iota(jnp.int32, (HI, peaks), 0).astype(jnp.float32).astype(jnp.bfloat16)
     lo_iota = lax.broadcasted_iota(jnp.int32, (LANES, peaks), 0).astype(jnp.float32).astype(jnp.bfloat16)
 
+    def fetches(c):
+        own = pl.ds(pl.multiple_of(c * CHUNK, CHUNK), CHUNK)
+        pairs = ((mass_any, mass_ref), (mobility_any, mobility_ref), (weight_any, weight_ref))
+        return [
+            pltpu.make_async_copy(src.at[own], dst.at[own], in_sem.at[c, k])
+            for k, (src, dst) in enumerate(pairs)
+        ]
+
     def spread(ref, p, count):
         return jnp.broadcast_to(ref[pl.ds(p, 1), :], (count, peaks)).astype(jnp.bfloat16)
 
-    def group(g, _):
-        base = pl.multiple_of(g * GROUP, GROUP)
-        for i in range(GROUP):
-            p = base + i
-            left = jnp.where(
-                spread(hi_ref, p, HI) == hi_iota, spread(value_ref, p, HI), jnp.bfloat16(0)
-            )
-            right = jnp.where(
-                spread(lo_ref, p, LANES) == lo_iota, jnp.bfloat16(1), jnp.bfloat16(0)
-            )
-            dense_ref[pl.ds(i, HI, stride=GROUP), :] = lax.dot_general(
-                left, right, (((1,), (1,)), ((), ())), preferred_element_type=jnp.float32
-            )
-        for h in range(HI):
-            out_ref[pl.ds(base, GROUP), h * LANES : (h + 1) * LANES] = dense_ref[
-                h * GROUP : (h + 1) * GROUP, :
-            ].astype(jnp.bfloat16)
+    for c in range(rows // CHUNK):
+        for copy in fetches(c):
+            copy.start()
+
+    def chunk(c, _):
+        for copy in fetches(c):
+            copy.wait()
+        start = pl.multiple_of(c * CHUNK, CHUNK)
+        own = pl.ds(start, CHUNK)
+        mass = mass_ref[own, :]
+        hi_ref[...] = (mobility_ref[own, :] * (MZ // LANES) + mass // LANES).astype(jnp.float32)
+        lo_ref[...] = (mass % LANES).astype(jnp.float32)
+        value_ref[...] = weight_ref[own, :].astype(jnp.float32)
+
+        def group(g, _):
+            base = pl.multiple_of(g * GROUP, GROUP)
+            for i in range(GROUP):
+                p = base + i
+                left = jnp.where(
+                    spread(hi_ref, p, HI) == hi_iota, spread(value_ref, p, HI), jnp.bfloat16(0)
+                )
+                right = jnp.where(
+                    spread(lo_ref, p, LANES) == lo_iota, jnp.bfloat16(1), jnp.bfloat16(0)
+                )
+                dense_ref[pl.ds(i, HI, stride=GROUP), :] = lax.dot_general(
+                    left, right, (((1,), (1,)), ((), ())), preferred_element_type=jnp.float32
+                )
+            for h in range(HI):
+                out_ref[pl.ds(start + base, GROUP), h * LANES : (h + 1) * LANES] = dense_ref[
+                    h * GROUP : (h + 1) * GROUP, :
+                ].astype(jnp.bfloat16)
+            return 0
+
+        lax.fori_loop(0, CHUNK // GROUP, group, 0)
         return 0
 
-    lax.fori_loop(0, rows // GROUP, group, 0)
-
-
-def bin_peaks(mass, mobility, weight):
-    rows, peaks = mass.shape
-    block = 128
-    spec = pl.BlockSpec((block, peaks), lambda i: (i, 0))
-    return pl.pallas_call(
-        bin_kernel,
-        out_shape=jax.ShapeDtypeStruct((rows, MZ * MOB), jnp.bfloat16),
-        grid=(rows // block,),
-        in_specs=[spec] * 3,
-        out_specs=pl.BlockSpec((block, MZ * MOB), lambda i: (i, 0)),
-        scratch_shapes=[pltpu.VMEM((block, peaks), jnp.float32)] * 3
-        + [pltpu.VMEM((HI * GROUP, LANES), jnp.float32)],
-        cost_estimate=pl.CostEstimate(
-            flops=2 * rows * peaks * MZ * MOB, bytes_accessed=rows * (peaks * 10 + MZ * MOB * 2), transcendentals=0
-        ),
-    )(mass, mobility, weight)
+    lax.fori_loop(0, rows // CHUNK, chunk, 0)
 
 
 def nmf_kernel(
-    pixes, chips, spectra_ref, basis_in, profiles_in, basis_ref, profiles_ref,
+    pixes, chips, mass_any, mobility_any, weight_any, basis_in, profiles_in, basis_ref, profiles_ref,
     pair_out, pair_in, gram_out, gram_in, chip_out, chip_in, pix_out, pix_in, whole_ref,
     rounded_ref, gram_h_out, gram_h_in, gram_h_pair_out, gram_h_pair_in, padded_ref,
     pair_sem, gram_sem, chip_sem, pix_sem, whole_sem, block_sem, block_pair_sem, gram_h_sem, gram_h_pair_sem,
+    spectra_ref, mass_ref, mobility_ref, weight_ref, hi_ref, lo_ref, value_ref, dense_ref, in_sem,
 ):
     rank, width = profiles_in.shape
     span = width // HALVES
@@ -95,6 +100,10 @@
     peers += [(pix_at(d), feat) for d in range(1, pixes)]
     for peer in peers:
         pl.semaphore_signal(barrier, inc=1, device_id=peer, device_id_type=pl.DeviceIdType.MESH)
+    bin_peaks(
+        mass_any, mobility_any, weight_any, spectra_ref, mass_ref, mobility_ref, weight_ref,
+        hi_ref, lo_ref, value_ref, dense_ref, in_sem,
+    )
     pl.semaphore_wait(barrier, len(peers))
 
     started = []
@@ -266,16 +275,17 @@
         copy.wait_send()
 
 
-def nmf(pixes, feats, spectra, basis, profiles):
+def nmf(pixes, feats, mass, mobility, weight, basis, profiles):
     rank, width = profiles.shape
     rows, span = basis.shape[1], width // HALVES
     chips, share = feats // 2, rank // pixes
     f32 = jnp.float32
+    peaks = mass.shape[1]
     dma = pltpu.SemaphoreType.DMA
     return pl.pallas_call(
         functools.partial(nmf_kernel, pixes, chips),
         out_shape=[jax.ShapeDtypeStruct(basis.shape, f32), jax.ShapeDtypeStruct(profiles.shape, f32)],
-        in_specs=[pl.BlockSpec(memory_space=pltpu.VMEM)] * 3,
+        in_specs=[pl.BlockSpec(memory_space=pl.ANY)] * 3 + [pl.BlockSpec(memory_space=pltpu.VMEM)] * 2,
         out_specs=[pl.BlockSpec(memory_space=pltpu.VMEM)] * 2,
         scratch_shapes=[
             pltpu.VMEM((ITERS, HALVES, chips, rank, span), f32),
@@ -302,19 +312,29 @@
             dma((ITERS, HALVES, chips, 2)),
             dma((ITERS, chips, 2)),
             dma((ITERS, 2)),
+            pltpu.VMEM((rows, MZ * MOB), jnp.bfloat16),
+            pltpu.VMEM((rows, peaks), jnp.int32),
+            pltpu.VMEM((rows, peaks), jnp.int32),
+            pltpu.VMEM((rows, peaks), jnp.bfloat16),
+            pltpu.VMEM((CHUNK, peaks), f32),
+            pltpu.VMEM((CHUNK, peaks), f32),
+            pltpu.VMEM((CHUNK, peaks), f32),
+            pltpu.VMEM((HI * GROUP, LANES), f32),
+            dma((rows // CHUNK, 3)),
         ],
         compiler_params=pltpu.CompilerParams(
             collective_id=0, has_side_effects=True, vmem_limit_bytes=44 * 1024 * 1024
         ),
-    )(spectra, basis, profiles)
+    )(mass, mobility, weight, basis, profiles)
 
 
 def solution(mesh):
     pixes, feats = mesh.shape["pix"], mesh.shape["feat"]
 
     def local(mass_bin, mobility_bin, intensity, basis_init, profile_init):
-        spectra = bin_peaks(mass_bin, mobility_bin, intensity)
-        basis, profiles = nmf(pixes, feats, spectra, basis_init.T, profile_init)
+        basis, profiles = nmf(
+            pixes, feats, mass_bin, mobility_bin, intensity, basis_init.T, profile_init
+        )
         return (basis.T, profiles)
 
     return jax.shard_map(

time: 106 us -> 108 us (1.019)
  local copies, waits for them, and re-layouts: 4.79 us -> 6.79 us
  Pallas kernels: 101 us -> 99.8 us
    pallas_call x1 -> x0, Pallas kernels: 33.9 us -> none  [bin_peaks(): pl.pallas_call(bin_kernel, out_shape=jax.ShapeDtypeStruct((rows, MZ * MOB...]
    pallas_call x1, Pallas kernels: 66.9 us -> 99.8 us  [nmf(): pl.pallas_call(functools.partial(nmf_kernel, pixes, chips), out_shape=[ja...]
    unnamed x8 -> x12, local copies, waits for them, and re-layouts: 4.79 us -> 6.79 us
where the time goes in v4:
time: 108 us; the launch traced here: 107 us
  Pallas kernels  99.8 us (92%)
  local copies, waits for them, and re-layouts  6.79 us (6%)
    pallas_call x1, Pallas kernels, nmf(): pl.pallas_call(functools.partial(nmf_kernel, pixes, chips), out_shape=[ja...  99.8 us
    unnamed x12, local copies, waits for them, and re-layouts  6.79 us

profile of v4, /device:TPU:0, one launch (start us, length us, event | category | flops | bytes accessed | tf_op | source)
XLA Modules:
  0.0 107.2 jit_solution(10816307761763312293)
XLA Ops:
  0.6 0.0 copy-start
  0.6 1.2 %copy-done = s32[1024,256]{1,0:T(8,128)S(1)} copy-done((s32[1024,256]{1,0:T(8,128)S(1)}, s32[1024,256]{1,0:T(8,128)}, u32[]{:S(2)}) %copy-start) | copy-done | bytes 1048600
  1.9 0.0 copy-start.1
  1.9 1.2 %copy-done.1 = s32[1024,256]{1,0:T(8,128)S(1)} copy-done((s32[1024,256]{1,0:T(8,128)S(1)}, s32[1024,256]{1,0:T(8,128)}, u32[]{:S(2)}) %copy-start.1) | copy-done | bytes 1048600
  3.1 0.0 copy-start.2
  3.1 1.0 copy-done.2
  4.1 0.0 copy-start.3
  4.1 0.9 copy-done.3
  5.1 0.0 copy-start.4
  5.1 0.9 copy-done.4
  6.0 99.8 %shard_map.68 = (f32[64,1024]{1,0:T(8,128)S(1)}, f32[64,1024]{1,0:T(8,128)S(1)}) custom-call(s32[1024,256]{1,0:T(8,128)S(1)} %copy-done, s32[1024,256]{1,0:T(8,128)S(1)} %copy-done.1, bf16[1024,256]{1,0:T(8,128)(2,1)S(1)} %copy-done.2, f32[64,1024]{1,0:T(8,128)S(1)} %bitcast.2, f32[64,1024]{1,0:T(8,128)S(1)} %copy-done.4), custom_call_target="tpu_custom_call" | custom-call | tf_op jit(solution)/shard_map/pallas_call | solution.py:285
  105.8 0.7 copy.9
  106.5 0.7 copy.10
Async XLA Ops:
  0.6 1.2 %copy-start = (s32[1024,256]{1,0:T(8,128)S(1)}, s32[1024,256]{1,0:T(8,128)}, u32[]{:S(2)}) copy-start(s32[1024,256]{1,0:T(8,128)} %mass_any.1) | copy-start | bytes 3145732
  1.9 1.2 %copy-start.1 = (s32[1024,256]{1,0:T(8,128)S(1)}, s32[1024,256]{1,0:T(8,128)}, u32[]{:S(2)}) copy-start(s32[1024,256]{1,0:T(8,128)} %mobility_any.1) | copy-start | bytes 3145732
  3.1 1.0 copy-start.2
  4.1 0.9 copy-start.3
  5.1 0.9 copy-start.4

commit v5 on v4

--- a/solution.py
+++ b/solution.py
@@ -50,17 +50,27 @@
 
         def group(g, _):
             base = pl.multiple_of(g * GROUP, GROUP)
-            for i in range(GROUP):
-                p = base + i
-                left = jnp.where(
-                    spread(hi_ref, p, HI) == hi_iota, spread(value_ref, p, HI), jnp.bfloat16(0)
-                )
-                right = jnp.where(
-                    spread(lo_ref, p, LANES) == lo_iota, jnp.bfloat16(1), jnp.bfloat16(0)
-                )
-                dense_ref[pl.ds(i, HI, stride=GROUP), :] = lax.dot_general(
-                    left, right, (((1,), (1,)), ((), ())), preferred_element_type=jnp.float32
-                )
+            for i in range(0, GROUP, 2):
+                left, right = [], []
+                for p in (base + i, base + i + 1):
+                    left.append(
+                        jnp.where(
+                            spread(hi_ref, p, HI) == hi_iota, spread(value_ref, p, HI), jnp.bfloat16(0)
+                        )
+                    )
+                    right.append(
+                        jnp.where(
+                            spread(lo_ref, p, LANES) == lo_iota, jnp.bfloat16(1), jnp.bfloat16(0)
+                        )
+                    )
+                both = lax.dot_general(
+                    jnp.concatenate(left, 0),
+                    jnp.concatenate(right, 0),
+                    (((1,), (1,)), ((), ())),
+                    preferred_element_type=jnp.float32,
+                )
+                dense_ref[pl.ds(i, HI, stride=GROUP), :] = both[:HI, :LANES]
+                dense_ref[pl.ds(i + 1, HI, stride=GROUP), :] = both[HI:, LANES:]
             for h in range(HI):
                 out_ref[pl.ds(start + base, GROUP), h * LANES : (h + 1) * LANES] = dense_ref[
                     h * GROUP : (h + 1) * GROUP, :
@@ -74,13 +84,14 @@
 
 
 def nmf_kernel(
-    pixes, chips, mass_any, mobility_any, weight_any, basis_in, profiles_in, basis_ref, profiles_ref,
+    pixes, chips, mass_any, mobility_any, weight_any, basis_any, profiles_any, basis_ref, profiles_ref,
     pair_out, pair_in, gram_out, gram_in, chip_out, chip_in, pix_out, pix_in, whole_ref,
     rounded_ref, gram_h_out, gram_h_in, gram_h_pair_out, gram_h_pair_in, padded_ref,
     pair_sem, gram_sem, chip_sem, pix_sem, whole_sem, block_sem, block_pair_sem, gram_h_sem, gram_h_pair_sem,
     spectra_ref, mass_ref, mobility_ref, weight_ref, hi_ref, lo_ref, value_ref, dense_ref, in_sem,
+    basis_in, profiles_in, start_sem,
 ):
-    rank, width = profiles_in.shape
+    rank, width = profiles_any.shape
     span = width // HALVES
     share = rank // pixes
     pix, feat = lax.axis_index("pix"), lax.axis_index("feat")
@@ -100,10 +111,18 @@
     peers += [(pix_at(d), feat) for d in range(1, pixes)]
     for peer in peers:
         pl.semaphore_signal(barrier, inc=1, device_id=peer, device_id_type=pl.DeviceIdType.MESH)
+    starts = [
+        pltpu.make_async_copy(basis_any, basis_in, start_sem.at[0]),
+        pltpu.make_async_copy(profiles_any, profiles_in, start_sem.at[1]),
+    ]
+    for copy in starts:
+        copy.start()
     bin_peaks(
         mass_any, mobility_any, weight_any, spectra_ref, mass_ref, mobility_ref, weight_ref,
         hi_ref, lo_ref, value_ref, dense_ref, in_sem,
     )
+    for copy in starts:
+        copy.wait()
     pl.semaphore_wait(barrier, len(peers))
 
     started = []
@@ -285,7 +304,7 @@
     return pl.pallas_call(
         functools.partial(nmf_kernel, pixes, chips),
         out_shape=[jax.ShapeDtypeStruct(basis.shape, f32), jax.ShapeDtypeStruct(profiles.shape, f32)],
-        in_specs=[pl.BlockSpec(memory_space=pl.ANY)] * 3 + [pl.BlockSpec(memory_space=pltpu.VMEM)] * 2,
+        in_specs=[pl.BlockSpec(memory_space=pltpu.HBM)] * 5,
         out_specs=[pl.BlockSpec(memory_space=pltpu.VMEM)] * 2,
         scratch_shapes=[
             pltpu.VMEM((ITERS, HALVES, chips, rank, span), f32),
@@ -321,6 +340,9 @@
             pltpu.VMEM((CHUNK, peaks), f32),
             pltpu.VMEM((HI * GROUP, LANES), f32),
             dma((rows // CHUNK, 3)),
+            pltpu.VMEM((rank, rows), f32),
+            pltpu.VMEM((rank, width), f32),
+            dma((2,)),
         ],
         compiler_params=pltpu.CompilerParams(
             collective_id=0, has_side_effects=True, vmem_limit_bytes=44 * 1024 * 1024

time: 108 us -> 107 us (level)
  no operation moved by 1% of the time
where the time goes in v5:
time: 107 us
  Pallas kernels  99.6 us (93%)
  local copies, waits for them, and re-layouts  6.79 us (6%)
    pallas_call x1, Pallas kernels, nmf(): pl.pallas_call(functools.partial(nmf_kernel, pixes, chips), out_shape=[ja...  99.6 us
    unnamed x12, local copies, waits for them, and re-layouts  6.79 us

profile of v5, /device:TPU:0, one launch (start us, length us, event | category | flops | bytes accessed | tf_op | source)
XLA Modules:
  0.0 107.1 jit_solution(10952486825064179580)
XLA Ops:
  0.6 0.0 copy-start
  0.6 1.2 %copy-done = s32[1024,256]{1,0:T(8,128)S(1)} copy-done((s32[1024,256]{1,0:T(8,128)S(1)}, s32[1024,256]{1,0:T(8,128)}, u32[]{:S(2)}) %copy-start) | copy-done | bytes 1048600
  1.9 0.0 copy-start.1
  1.9 1.2 %copy-done.1 = s32[1024,256]{1,0:T(8,128)S(1)} copy-done((s32[1024,256]{1,0:T(8,128)S(1)}, s32[1024,256]{1,0:T(8,128)}, u32[]{:S(2)}) %copy-start.1) | copy-done | bytes 1048600
  3.1 0.0 copy-start.2
  3.1 1.0 copy-done.2
  4.1 0.0 copy-start.3
  4.1 0.9 copy-done.3
  5.1 0.0 copy-start.4
  5.1 0.9 copy-done.4
  6.0 99.6 %shard_map.68 = (f32[64,1024]{1,0:T(8,128)S(1)}, f32[64,1024]{1,0:T(8,128)S(1)}) custom-call(s32[1024,256]{1,0:T(8,128)S(1)} %copy-done, s32[1024,256]{1,0:T(8,128)S(1)} %copy-done.1, bf16[1024,256]{1,0:T(8,128)(2,1)S(1)} %copy-done.2, f32[64,1024]{1,0:T(8,128)S(1)} %bitcast.2, f32[64,1024]{1,0:T(8,128)S(1)} %copy-done.4), custom_call_target="tpu_custom_call" | custom-call | tf_op jit(solution)/shard_map/pallas_call | solution.py:304
  105.6 0.7 copy.9
  106.4 0.7 copy.10
Async XLA Ops:
  0.6 1.2 %copy-start = (s32[1024,256]{1,0:T(8,128)S(1)}, s32[1024,256]{1,0:T(8,128)}, u32[]{:S(2)}) copy-start(s32[1024,256]{1,0:T(8,128)} %mass_any.1) | copy-start | bytes 3145732
  1.9 1.2 %copy-start.1 = (s32[1024,256]{1,0:T(8,128)S(1)}, s32[1024,256]{1,0:T(8,128)}, u32[]{:S(2)}) copy-start(s32[1024,256]{1,0:T(8,128)} %mobility_any.1) | copy-start | bytes 3145732
  3.1 1.0 copy-start.2
  4.1 0.9 copy-start.3
  5.1 0.9 copy-start.4

commit v6 on v5

--- a/solution.py
+++ b/solution.py
@@ -58,11 +58,8 @@
                             spread(hi_ref, p, HI) == hi_iota, spread(value_ref, p, HI), jnp.bfloat16(0)
                         )
                     )
-                    right.append(
-                        jnp.where(
-                            spread(lo_ref, p, LANES) == lo_iota, jnp.bfloat16(1), jnp.bfloat16(0)
-                        )
-                    )
+                    away = spread(lo_ref, p, LANES) - lo_iota
+                    right.append(jnp.maximum(jnp.bfloat16(1) - away * away, jnp.bfloat16(0)))
                 both = lax.dot_general(
                     jnp.concatenate(left, 0),
                     jnp.concatenate(right, 0),
@@ -345,7 +342,7 @@
             dma((2,)),
         ],
         compiler_params=pltpu.CompilerParams(
-            collective_id=0, has_side_effects=True, vmem_limit_bytes=44 * 1024 * 1024
+            collective_id=0, has_side_effects=True, vmem_limit_bytes=63 * 1024 * 1024
         ),
     )(mass, mobility, weight, basis, profiles)
 

time: 107 us -> 101 us (0.944)
  local copies, waits for them, and re-layouts: 6.79 us -> 2.42 us
  Pallas kernels: 99.6 us -> 97.8 us
    unnamed x12 -> x4, local copies, waits for them, and re-layouts: 6.79 us -> 2.42 us
    pallas_call x1, Pallas kernels: 99.6 us -> 97.8 us  [nmf(): pl.pallas_call(functools.partial(nmf_kernel, pixes, chips), out_shape=[ja...]
where the time goes in v6:
time: 101 us
  Pallas kernels  97.8 us (97%)
  local copies, waits for them, and re-layouts  2.42 us (2%)
    pallas_call x1, Pallas kernels, nmf(): pl.pallas_call(functools.partial(nmf_kernel, pixes, chips), out_shape=[ja...  97.8 us
    unnamed x4, local copies, waits for them, and re-layouts  2.42 us

profile of v6, /device:TPU:0, one launch (start us, length us, event | category | flops | bytes accessed | tf_op | source)
XLA Modules:
  0.0 100.9 jit_solution(11259626044121399947)
XLA Ops:
  0.6 97.8 %shard_map.68 = (f32[64,1024]{1,0:T(8,128)}, f32[64,1024]{1,0:T(8,128)}) custom-call(s32[1024,256]{1,0:T(8,128)} %mass_any.1, s32[1024,256]{1,0:T(8,128)} %mobility_any.1, bf16[1024,256]{1,0:T(8,128)(2,1)} %weight_any.1, f32[64,1024]{1,0:T(8,128)} %bitcast.2, f32[64,1024]{1,0:T(8,128)} %profiles_any.1), custom_call_target="tpu_custom_call" | custom-call | tf_op jit(solution)/shard_map/pallas_call | solution.py:301
  98.5 0.0 copy-start
  98.5 1.7 %copy.9 = f32[1024,64]{0,1:T(8,128)} copy(f32[1024,64]{0,1:T(8,128)} %bitcast.3) | data formatting | bytes 524288
  100.2 0.0 copy-done
  100.2 0.7 copy.10
Async XLA Ops:
  98.5 1.7 %copy-start = (f32[64,1024]{1,0:T(8,128)S(1)}, f32[64,1024]{1,0:T(8,128)}, u32[]{:S(2)}) copy-start(f32[64,1024]{1,0:T(8,128)} %get-tuple-element.9) | copy-start | bytes 786436

commit v7 on v6

--- a/solution.py
+++ b/solution.py
@@ -12,13 +12,14 @@
 MOB = 16
 HI = MZ * MOB // LANES
 GROUP = 16
+UNROLL = 4
 CHUNK = 128
 ITERS = 2
 HALVES = 2
 EPS = 1e-06
 
 
-def bin_peaks(mass_any, mobility_any, weight_any, out_ref, mass_ref, mobility_ref, weight_ref, hi_ref, lo_ref, value_ref, dense_ref, in_sem):
+def bin_peaks(mass_any, mobility_any, weight_any, out_ref, mass_ref, mobility_ref, weight_ref, hi_ref, lo_ref, value_ref, dense_refs, in_sem):
     rows, peaks = mass_any.shape
     hi_iota = lax.broadcasted_iota(jnp.int32, (HI, peaks), 0).astype(jnp.float32).astype(jnp.bfloat16)
     lo_iota = lax.broadcasted_iota(jnp.int32, (LANES, peaks), 0).astype(jnp.float32).astype(jnp.bfloat16)
@@ -49,32 +50,33 @@
         value_ref[...] = weight_ref[own, :].astype(jnp.float32)
 
         def group(g, _):
-            base = pl.multiple_of(g * GROUP, GROUP)
-            for i in range(0, GROUP, 2):
-                left, right = [], []
-                for p in (base + i, base + i + 1):
-                    left.append(
-                        jnp.where(
-                            spread(hi_ref, p, HI) == hi_iota, spread(value_ref, p, HI), jnp.bfloat16(0)
+            base = pl.multiple_of(g * GROUP * UNROLL, GROUP * UNROLL)
+            for u in range(UNROLL):
+                for i in range(0, GROUP, 2):
+                    left, right = [], []
+                    for p in (base + u * GROUP + i, base + u * GROUP + i + 1):
+                        left.append(
+                            jnp.where(
+                                spread(hi_ref, p, HI) == hi_iota, spread(value_ref, p, HI), jnp.bfloat16(0)
+                            )
                         )
+                        away = spread(lo_ref, p, LANES) - lo_iota
+                        right.append(jnp.maximum(jnp.bfloat16(1) - away * away, jnp.bfloat16(0)))
+                    both = lax.dot_general(
+                        jnp.concatenate(left, 0),
+                        jnp.concatenate(right, 0),
+                        (((1,), (1,)), ((), ())),
+                        preferred_element_type=jnp.float32,
                     )
-                    away = spread(lo_ref, p, LANES) - lo_iota
-                    right.append(jnp.maximum(jnp.bfloat16(1) - away * away, jnp.bfloat16(0)))
-                both = lax.dot_general(
-                    jnp.concatenate(left, 0),
-                    jnp.concatenate(right, 0),
-                    (((1,), (1,)), ((), ())),
-                    preferred_element_type=jnp.float32,
-                )
-                dense_ref[pl.ds(i, HI, stride=GROUP), :] = both[:HI, :LANES]
-                dense_ref[pl.ds(i + 1, HI, stride=GROUP), :] = both[HI:, LANES:]
-            for h in range(HI):
-                out_ref[pl.ds(start + base, GROUP), h * LANES : (h + 1) * LANES] = dense_ref[
-                    h * GROUP : (h + 1) * GROUP, :
-                ].astype(jnp.bfloat16)
+                    dense_refs[u][pl.ds(i, HI, stride=GROUP), :] = both[:HI, :LANES]
+                    dense_refs[u][pl.ds(i + 1, HI, stride=GROUP), :] = both[HI:, LANES:]
+                for h in range(HI):
+                    out_ref[pl.ds(start + base + u * GROUP, GROUP), h * LANES : (h + 1) * LANES] = dense_refs[u][
+                        h * GROUP : (h + 1) * GROUP, :
+                    ].astype(jnp.bfloat16)
             return 0
 
-        lax.fori_loop(0, CHUNK // GROUP, group, 0)
+        lax.fori_loop(0, CHUNK // (GROUP * UNROLL), group, 0)
         return 0
 
     lax.fori_loop(0, rows // CHUNK, chunk, 0)
@@ -85,7 +87,7 @@
     pair_out, pair_in, gram_out, gram_in, chip_out, chip_in, pix_out, pix_in, whole_ref,
     rounded_ref, gram_h_out, gram_h_in, gram_h_pair_out, gram_h_pair_in, padded_ref,
     pair_sem, gram_sem, chip_sem, pix_sem, whole_sem, block_sem, block_pair_sem, gram_h_sem, gram_h_pair_sem,
-    spectra_ref, mass_ref, mobility_ref, weight_ref, hi_ref, lo_ref, value_ref, dense_ref, in_sem,
+    spectra_ref, mass_ref, mobility_ref, weight_ref, hi_ref, lo_ref, value_ref, dense_a, dense_b, dense_c, dense_d, in_sem,
     basis_in, profiles_in, start_sem,
 ):
     rank, width = profiles_any.shape
@@ -116,7 +118,7 @@
         copy.start()
     bin_peaks(
         mass_any, mobility_any, weight_any, spectra_ref, mass_ref, mobility_ref, weight_ref,
-        hi_ref, lo_ref, value_ref, dense_ref, in_sem,
+        hi_ref, lo_ref, value_ref, (dense_a, dense_b, dense_c, dense_d), in_sem,
     )
     for copy in starts:
         copy.wait()
@@ -336,6 +338,9 @@
             pltpu.VMEM((CHUNK, peaks), f32),
             pltpu.VMEM((CHUNK, peaks), f32),
             pltpu.VMEM((HI * GROUP, LANES), f32),
+            pltpu.VMEM((HI * GROUP, LANES), f32),
+            pltpu.VMEM((HI * GROUP, LANES), f32),
+            pltpu.VMEM((HI * GROUP, LANES), f32),
             dma((rows // CHUNK, 3)),
             pltpu.VMEM((rank, rows), f32),
             pltpu.VMEM((rank, width), f32),

time: 101 us -> 94.4 us (0.935)
  Pallas kernels: 97.8 us -> 91.2 us
    pallas_call x1, Pallas kernels: 97.8 us -> 91.2 us  [nmf(): pl.pallas_call(functools.partial(nmf_kernel, pixes, chips), out_shape=[ja...]
where the time goes in v7:
time: 94.4 us; the launch traced here: 94.3 us
  Pallas kernels  91.2 us (97%)
  local copies, waits for them, and re-layouts  2.42 us (3%)
    pallas_call x1, Pallas kernels, nmf(): pl.pallas_call(functools.partial(nmf_kernel, pixes, chips), out_shape=[ja...  91.2 us
    unnamed x4, local copies, waits for them, and re-layouts  2.42 us

profile of v7, /device:TPU:0, one launch (start us, length us, event | category | flops | bytes accessed | tf_op | source)
XLA Modules:
  0.0 94.3 jit_solution(9947161552711830584)
XLA Ops:
  0.6 91.2 %shard_map.68 = (f32[64,1024]{1,0:T(8,128)}, f32[64,1024]{1,0:T(8,128)}) custom-call(s32[1024,256]{1,0:T(8,128)} %mass_any.1, s32[1024,256]{1,0:T(8,128)} %mobility_any.1, bf16[1024,256]{1,0:T(8,128)(2,1)} %weight_any.1, f32[64,1024]{1,0:T(8,128)} %bitcast.2, f32[64,1024]{1,0:T(8,128)} %profiles_any.1), custom_call_target="tpu_custom_call" | custom-call | tf_op jit(solution)/shard_map/pallas_call | solution.py:303
  91.8 0.0 copy-start
  91.9 1.7 %copy.9 = f32[1024,64]{0,1:T(8,128)} copy(f32[1024,64]{0,1:T(8,128)} %bitcast.3) | data formatting | bytes 524288
  93.6 0.0 copy-done
  93.6 0.7 copy.10
Async XLA Ops:
  91.8 1.7 %copy-start = (f32[64,1024]{1,0:T(8,128)S(1)}, f32[64,1024]{1,0:T(8,128)}, u32[]{:S(2)}) copy-start(f32[64,1024]{1,0:T(8,128)} %get-tuple-element.9) | copy-start | bytes 786436

commit v8 on v7

--- a/solution.py
+++ b/solution.py
@@ -15,7 +15,7 @@
 UNROLL = 4
 CHUNK = 128
 ITERS = 2
-HALVES = 2
+HALVES = 4
 EPS = 1e-06
 
 

time: 94.4 us -> 94.4 us (level)
  no operation moved by 1% of the time
where the time goes in v8:
time: 94.4 us; the launch traced here: 94.2 us
  Pallas kernels  91.2 us (97%)
  local copies, waits for them, and re-layouts  2.42 us (3%)
    pallas_call x1, Pallas kernels, nmf(): pl.pallas_call(functools.partial(nmf_kernel, pixes, chips), out_shape=[ja...  91.2 us
    unnamed x4, local copies, waits for them, and re-layouts  2.42 us

profile of v8, /device:TPU:0, one launch (start us, length us, event | category | flops | bytes accessed | tf_op | source)
XLA Modules:
  0.0 94.2 jit_solution(7182303017356930905)
XLA Ops:
  0.6 91.2 %shard_map.68 = (f32[64,1024]{1,0:T(8,128)}, f32[64,1024]{1,0:T(8,128)}) custom-call(s32[1024,256]{1,0:T(8,128)} %mass_any.1, s32[1024,256]{1,0:T(8,128)} %mobility_any.1, bf16[1024,256]{1,0:T(8,128)(2,1)} %weight_any.1, f32[64,1024]{1,0:T(8,128)} %bitcast.2, f32[64,1024]{1,0:T(8,128)} %profiles_any.1), custom_call_target="tpu_custom_call" | custom-call | tf_op jit(solution)/shard_map/pallas_call | solution.py:303
  91.8 0.0 copy-start
  91.8 1.7 %copy.9 = f32[1024,64]{0,1:T(8,128)} copy(f32[1024,64]{0,1:T(8,128)} %bitcast.3) | data formatting | bytes 524288
  93.5 0.0 copy-done
  93.5 0.7 copy.10
Async XLA Ops:
  91.8 1.7 %copy-start = (f32[64,1024]{1,0:T(8,128)S(1)}, f32[64,1024]{1,0:T(8,128)}, u32[]{:S(2)}) copy-start(f32[64,1024]{1,0:T(8,128)} %get-tuple-element.9) | copy-start | bytes 786436
